TPU v7x, 512 devices: a whole 4x8x8 slice. The times are simulated.
512 devices in a mesh: blk: 64 (over x, z, core), uly: 8 (over y).
Axes of the slice: x: 4, y: 8, z: 8, core: 2. Of those that a mesh axis runs over, the one named last changes fastest.
Arguments:
- queries: bfloat16 [49152, 3072], P(('blk', 'uly')), may hold values from -23 to 23
- keys: bfloat16 [49152, 3072], P(('blk', 'uly')), may hold values from -4.5 to 4.5
- values: bfloat16 [49152, 3072], P(('blk', 'uly')), may hold values from -4.5 to 4.5
- key_lists: int32 [384, 16], P('blk'), may hold values from 0 to 383, as said below
- key_fill: int32 [384], replicated, may hold values from 48 to 96
Outputs:
- attended: bfloat16 [49152, 3072], P(('blk', 'uly'))
Inputs may be any that keep to these rules, and one draw needn't show every extreme that they name: `key_lists`: the rows of one aligned block of 3 query tiles (one query cluster) are equal; within a row the tiles t have distinct t // 6; among the rows of one aligned block of 6 query tiles, tiles with equal t // 6 are equal.
All inputs are finite; a program needn't handle non-finite values.
Results may differ from a plain program's by a relative error of at most 0.0047.
Values may be sent and summed in bfloat16 or wider, within the bound.
A program may use at most 128 MiB of HBM per device.

v0:
```python
import math

import jax
import jax.numpy as jnp
from jax import lax
from jax.sharding import PartitionSpec as P

HD = 128
TILE = 128
SEL = 16


def local(queries, keys, values, key_lists, key_fill):
    head_queries, head_keys, head_values = (
        lax.all_to_all(queries, "uly", split_axis=1, concat_axis=0, tiled=True),
        lax.all_to_all(keys, "uly", split_axis=1, concat_axis=0, tiled=True),
        lax.all_to_all(values, "uly", split_axis=1, concat_axis=0, tiled=True),
    )
    row_count, feature_width = head_queries.shape
    head_count = feature_width // HD
    blocks = lax.axis_size("blk")
    per_owner = row_count // TILE
    owner_index = lax.axis_index("blk")
    local_tiles = key_lists.shape[0]
    all_lists = lax.all_gather(key_lists, "blk", axis=0, tiled=True)
    wanted_tiles = all_lists.reshape(blocks, local_tiles * SEL)
    from_owner = wanted_tiles // per_owner == owner_index
    wanted = jnp.max(jnp.where(from_owner, wanted_tiles - owner_index * per_owner, 0), axis=1)
    key_stack = head_keys.reshape(per_owner, TILE, feature_width)
    value_stack = head_values.reshape(per_owner, TILE, feature_width)
    sent_keys = key_stack[wanted]
    sent_values = value_stack[wanted]
    got_keys, got_values = (
        lax.all_to_all(sent_keys, "blk", split_axis=0, concat_axis=0, tiled=True),
        lax.all_to_all(sent_values, "blk", split_axis=0, concat_axis=0, tiled=True),
    )
    slot_depth = got_keys.shape[1]
    got_keys = got_keys.reshape(blocks, slot_depth, head_count, HD)
    got_values = got_values.reshape(blocks, slot_depth, head_count, HD)
    query_tiles = head_queries.reshape(local_tiles, TILE, head_count, HD)
    columns = jnp.arange(slot_depth, dtype=jnp.int32)
    score_scale = 1.0 / math.sqrt(HD)

    def attend(tile_pair):
        query_tile, tile_list = tile_pair
        slot_index = tile_list // per_owner
        picked_keys = got_keys[slot_index]
        picked_values = got_values[slot_index]
        live_mask = columns[None, :] < key_fill[tile_list][:, None]
        scores = (
            jnp.einsum(
                "qhd,sthd->hqst", query_tile, picked_keys, preferred_element_type=jnp.float32
            )
            * score_scale
        )
        scores = jnp.where(live_mask[None, None], scores, -1e30)
        peak = jnp.max(scores, axis=(2, 3), keepdims=True)
        weight_raw = jnp.where(live_mask[None, None], jnp.exp(scores - peak), 0.0)
        row_total = jnp.sum(weight_raw, axis=(2, 3))
        weight = weight_raw.astype(jnp.bfloat16)
        mixture = jnp.einsum(
            "hqst,sthd->qhd", weight, picked_values, preferred_element_type=jnp.float32
        )
        result = mixture / jnp.transpose(row_total)[:, :, None]
        return result.astype(jnp.bfloat16).reshape(TILE, feature_width)

    attended = lax.map(attend, (query_tiles, key_lists)).reshape(row_count, feature_width)
    return lax.all_to_all(attended, "uly", split_axis=0, concat_axis=1, tiled=True)


def solution(mesh):
    in_specs = (
        P(("blk", "uly"), None),
        P(("blk", "uly"), None),
        P(("blk", "uly"), None),
        P("blk", None),
        P(),
    )
    out_specs = P(("blk", "uly"), None)
    return jax.shard_map(local, mesh=mesh, in_specs=in_specs, out_specs=out_specs, check_vma=False)
```

profile of v0, /device:TPU:1, one launch (start us, length us, event | category | flops | bytes accessed | tf_op | source)
XLA Modules:
  0.0 570.8 jit_solution(15221102016552087221)
XLA Ops:
  0.0 2.0 copy.84
  2.0 7.7 %all-to-all-start = ((bf16[96,8,384]{2,0,1:T(8,128)(2,1)}), bf16[96,8,384]{2,0,1:T(8,128)(2,1)S(1)}, u32[]{:S(2)}, u32[]{:S(2)}) async-start(bf16[96,8,384]{2,0,1:T(8,128)(2,1)} %bitcast.73), calls=%async_computation | async-start | bytes 1179648 | tf_op jit(solution)/shard_map/all_to_all | solution.py:17
  9.7 1.9 copy.82
  11.6 14.5 %all-to-all-done = bf16[96,8,384]{2,0,1:T(8,128)(2,1)S(1)} async-done(((bf16[96,8,384]{2,0,1:T(8,128)(2,1)}), bf16[96,8,384]{2,0,1:T(8,128)(2,1)S(1)}, u32[]{:S(2)}, u32[]{:S(2)}) %all-to-all-start) | async-done | bytes 589856 | tf_op jit(solution)/shard_map/all_to_all | solution.py:17
  26.1 3.5 all-to-all-start.3
  29.7 53.5 %all-gather = s32[64,6,16]{2,1,0:T(8,128)S(1)} all-gather(s32[1,6,16]{2,1,0:T(8,128)S(1)} %bitcast.109), channel_id=1, replica_groups=mesh['blk'=64,'uly'=8] {'blk'}, dimensions={0}, use_global_device_ids=true | all-gather | bytes 24960 | tf_op jit(solution)/shard_map/all_gather | solution.py:25
  83.3 0.9 copy.83
  84.2 6.8 %all-to-all-start.2 = ((bf16[96,8,384]{2,0,1:T(8,128)(2,1)}), bf16[96,8,384]{2,0,1:T(8,128)(2,1)S(1)}, u32[]{:S(2)}, u32[]{:S(2)}) async-start(bf16[96,8,384]{2,0,1:T(8,128)(2,1)} %bitcast.72), calls=%async_computation.2 | async-start | bytes 1179648 | tf_op jit(solution)/shard_map/all_to_all | solution.py:15
  92.0 4.1 gather_fusion.3
  96.1 14.3 %all-to-all-done.2 = bf16[96,8,384]{2,0,1:T(8,128)(2,1)S(1)} async-done(((bf16[96,8,384]{2,0,1:T(8,128)(2,1)}), bf16[96,8,384]{2,0,1:T(8,128)(2,1)S(1)}, u32[]{:S(2)}, u32[]{:S(2)}) %all-to-all-start.2) | async-done | bytes 589856 | tf_op jit(solution)/shard_map/all_to_all | solution.py:15
  110.4 5.8 %all-to-all-start.1 = ((bf16[64,128,384]{2,1,0:T(8,128)(2,1)}), bf16[64,128,384]{2,1,0:T(8,128)(2,1)}, u32[]{:S(2)}, u32[]{:S(2)}) async-start(bf16[64,128,384]{2,1,0:T(8,128)(2,1)} %gather_fusion.3), calls=%async_computation.1 | async-start | bytes 12582912 | tf_op jit(solution)/shard_map/all_to_all | solution.py:35
  116.2 4.0 gather_fusion.4
  120.2 136.9 %all-to-all-done.1 = bf16[64,128,384]{2,1,0:T(8,128)(2,1)} async-done(((bf16[64,128,384]{2,1,0:T(8,128)(2,1)}), bf16[64,128,384]{2,1,0:T(8,128)(2,1)}, u32[]{:S(2)}, u32[]{:S(2)}) %all-to-all-start.1) | async-done | bytes 6291488 | tf_op jit(solution)/shard_map/all_to_all | solution.py:35
  257.1 6.0 %all-to-all-start.4 = ((bf16[64,128,384]{2,1,0:T(8,128)(2,1)}), bf16[64,128,384]{2,1,0:T(8,128)(2,1)}, u32[]{:S(2)}, u32[]{:S(2)}) async-start(bf16[64,128,384]{2,1,0:T(8,128)(2,1)} %gather_fusion.4), calls=%async_computation.4 | async-start | bytes 12582912 | tf_op jit(solution)/shard_map/all_to_all | solution.py:34
  263.3 1.0 copy.59
  264.2 8.6 %copy.54 = bf16[64,128,384]{1,2,0:T(8,128)(2,1)} copy(bf16[64,128,384]{2,1,0:T(8,128)(2,1)} %all-to-all-done.1) | data formatting | bytes 12582912 | tf_op jit(solution)/shard_map/all_to_all | solution.py:35
  272.9 13.1 %copy.58 = bf16[64,128,3,128]{3,2,1,0:T(4,128)(2,1)} copy(bf16[64,128,3,128]{1,3,2,0:T(8,128)(2,1)} %bitcast.99) | data formatting | bytes 12582912
  286.0 117.9 %all-to-all-done.4 = bf16[64,128,384]{2,1,0:T(8,128)(2,1)} async-done(((bf16[64,128,384]{2,1,0:T(8,128)(2,1)}), bf16[64,128,384]{2,1,0:T(8,128)(2,1)}, u32[]{:S(2)}, u32[]{:S(2)}) %all-to-all-start.4) | async-done | bytes 6291488 | tf_op jit(solution)/shard_map/all_to_all | solution.py:34
  403.9 8.6 %copy.57 = bf16[64,128,384]{1,2,0:T(8,128)(2,1)} copy(bf16[64,128,384]{2,1,0:T(8,128)(2,1)} %all-to-all-done.4) | data formatting | bytes 12582912 | tf_op jit(solution)/shard_map/all_to_all | solution.py:34
  412.5 13.1 %copy.60 = bf16[64,128,3,128]{3,2,1,0:T(4,128)(2,1)} copy(bf16[64,128,3,128]{1,3,2,0:T(8,128)(2,1)} %bitcast.100) | data formatting | bytes 12582912
  425.6 121.5 %while.13 = (s32[]{:T(128)}, bf16[6,128,384]{2,1,0:T(8,128)(2,1)}, s32[6,16]{1,0:T(8,128)S(1)}, bf16[64,128,3,128]{3,2,1,0:T(4,128)(2,1)}, s32[384]{0:T(512)S(1)...) while((s32[]{:T(128)}, bf16[6,128,384]{2,1,0:T(8,128)(2,1)}, ...), condition=%wide.region_5.6_spmd.clone, body=%wide.region_2.5_spmd.clone.sunk | while | flops 412978656 | bytes 22635800 | solution.py:67
  425.6 0.7 gather_fusion
  426.4 5.7 %gather_fusion.1 = bf16[16,128,3,128]{3,2,1,0:T(4,128)(2,1)S(1)} fusion(bf16[64,128,3,128]{3,2,1,0:T(4,128)(2,1)} %get-tuple-element.249, s32[1024]{0:T(1024)S(1)} %get-tuple-element.224), kind=kCustom, calls=%fused_computation.2.clone.clone.1 | custom fusion | bytes 3145792 | tf_op jit(solution)/shard_map/while/body/eval_jaxpr/gather | solution.py:47
  432.6 1.6 fusion.52
  434.2 0.9 fusion.53
  435.1 7.0 %gather_fusion.2 = bf16[16,128,3,128]{3,2,1,0:T(4,128)(2,1)} fusion(bf16[64,128,3,128]{3,2,1,0:T(4,128)(2,1)} %get-tuple-element.246, s32[1024]{0:T(1024)S(1)} %get-tuple-element.224), kind=kCustom, calls=%fused_computation.clone.clone.1 | custom fusion | bytes 3145792 | tf_op jit(solution)/shard_map/while/body/eval_jaxpr/gather | solution.py:48
  442.1 3.0 fusion.54
  445.2 0.7 constant_dynamic-update-slice_fusion.2
  445.9 0.7 gather_fusion
  446.6 5.7 %gather_fusion.1 = bf16[16,128,3,128]{3,2,1,0:T(4,128)(2,1)S(1)} fusion(bf16[64,128,3,128]{3,2,1,0:T(4,128)(2,1)} %get-tuple-element.249, s32[1024]{0:T(1024)S(1)} %get-tuple-element.224), kind=kCustom, calls=%fused_computation.2.clone.clone.1 | custom fusion | bytes 3145792 | tf_op jit(solution)/shard_map/while/body/eval_jaxpr/gather | solution.py:47
  452.8 1.6 fusion.52
  454.4 0.9 fusion.53
  455.4 7.0 %gather_fusion.2 = bf16[16,128,3,128]{3,2,1,0:T(4,128)(2,1)} fusion(bf16[64,128,3,128]{3,2,1,0:T(4,128)(2,1)} %get-tuple-element.246, s32[1024]{0:T(1024)S(1)} %get-tuple-element.224), kind=kCustom, calls=%fused_computation.clone.clone.1 | custom fusion | bytes 3145792 | tf_op jit(solution)/shard_map/while/body/eval_jaxpr/gather | solution.py:48
  462.3 3.0 fusion.54
  465.4 0.7 constant_dynamic-update-slice_fusion.2
  466.1 0.7 gather_fusion
  466.9 5.7 %gather_fusion.1 = bf16[16,128,3,128]{3,2,1,0:T(4,128)(2,1)S(1)} fusion(bf16[64,128,3,128]{3,2,1,0:T(4,128)(2,1)} %get-tuple-element.249, s32[1024]{0:T(1024)S(1)} %get-tuple-element.224), kind=kCustom, calls=%fused_computation.2.clone.clone.1 | custom fusion | bytes 3145792 | tf_op jit(solution)/shard_map/while/body/eval_jaxpr/gather | solution.py:47
  473.0 1.6 fusion.52
  474.7 0.9 fusion.53
  475.6 7.0 %gather_fusion.2 = bf16[16,128,3,128]{3,2,1,0:T(4,128)(2,1)} fusion(bf16[64,128,3,128]{3,2,1,0:T(4,128)(2,1)} %get-tuple-element.246, s32[1024]{0:T(1024)S(1)} %get-tuple-element.224), kind=kCustom, calls=%fused_computation.clone.clone.1 | custom fusion | bytes 3145792 | tf_op jit(solution)/shard_map/while/body/eval_jaxpr/gather | solution.py:48
  482.6 3.0 fusion.54
  485.7 0.7 constant_dynamic-update-slice_fusion.2
  486.4 0.7 gather_fusion
  487.1 5.7 %gather_fusion.1 = bf16[16,128,3,128]{3,2,1,0:T(4,128)(2,1)S(1)} fusion(bf16[64,128,3,128]{3,2,1,0:T(4,128)(2,1)} %get-tuple-element.249, s32[1024]{0:T(1024)S(1)} %get-tuple-element.224), kind=kCustom, calls=%fused_computation.2.clone.clone.1 | custom fusion | bytes 3145792 | tf_op jit(solution)/shard_map/while/body/eval_jaxpr/gather | solution.py:47
  493.3 1.6 fusion.52
  494.9 0.9 fusion.53
  495.9 7.0 %gather_fusion.2 = bf16[16,128,3,128]{3,2,1,0:T(4,128)(2,1)} fusion(bf16[64,128,3,128]{3,2,1,0:T(4,128)(2,1)} %get-tuple-element.246, s32[1024]{0:T(1024)S(1)} %get-tuple-element.224), kind=kCustom, calls=%fused_computation.clone.clone.1 | custom fusion | bytes 3145792 | tf_op jit(solution)/shard_map/while/body/eval_jaxpr/gather | solution.py:48
  502.8 3.0 fusion.54
  505.9 0.7 constant_dynamic-update-slice_fusion.2
  506.6 0.7 gather_fusion
  507.4 5.7 %gather_fusion.1 = bf16[16,128,3,128]{3,2,1,0:T(4,128)(2,1)S(1)} fusion(bf16[64,128,3,128]{3,2,1,0:T(4,128)(2,1)} %get-tuple-element.249, s32[1024]{0:T(1024)S(1)} %get-tuple-element.224), kind=kCustom, calls=%fused_computation.2.clone.clone.1 | custom fusion | bytes 3145792 | tf_op jit(solution)/shard_map/while/body/eval_jaxpr/gather | solution.py:47
  513.5 1.6 fusion.52
  515.2 0.9 fusion.53
  516.1 7.0 %gather_fusion.2 = bf16[16,128,3,128]{3,2,1,0:T(4,128)(2,1)} fusion(bf16[64,128,3,128]{3,2,1,0:T(4,128)(2,1)} %get-tuple-element.246, s32[1024]{0:T(1024)S(1)} %get-tuple-element.224), kind=kCustom, calls=%fused_computation.clone.clone.1 | custom fusion | bytes 3145792 | tf_op jit(solution)/shard_map/while/body/eval_jaxpr/gather | solution.py:48
  523.1 3.0 fusion.54
  526.2 0.7 constant_dynamic-update-slice_fusion.2
  526.9 0.7 gather_fusion
  527.6 5.7 %gather_fusion.1 = bf16[16,128,3,128]{3,2,1,0:T(4,128)(2,1)S(1)} fusion(bf16[64,128,3,128]{3,2,1,0:T(4,128)(2,1)} %get-tuple-element.249, s32[1024]{0:T(1024)S(1)} %get-tuple-element.224), kind=kCustom, calls=%fused_computation.2.clone.clone.1 | custom fusion | bytes 3145792 | tf_op jit(solution)/shard_map/while/body/eval_jaxpr/gather | solution.py:47
  533.8 1.6 fusion.52
  535.4 0.9 fusion.53
  536.4 7.0 %gather_fusion.2 = bf16[16,128,3,128]{3,2,1,0:T(4,128)(2,1)} fusion(bf16[64,128,3,128]{3,2,1,0:T(4,128)(2,1)} %get-tuple-element.246, s32[1024]{0:T(1024)S(1)} %get-tuple-element.224), kind=kCustom, calls=%fused_computation.clone.clone.1 | custom fusion | bytes 3145792 | tf_op jit(solution)/shard_map/while/body/eval_jaxpr/gather | solution.py:48
  543.3 3.0 fusion.54
  547.1 22.9 %all_to_all.77 = bf16[8,96,384]{2,1,0:T(8,128)(2,1)S(1)} all-to-all(bf16[8,96,384]{2,1,0:T(8,128)(2,1)} %bitcast.107), channel_id=1, replica_groups=mesh['blk'=64,'uly'=8] {'uly'}, dimensions={0} | all-to-all | bytes 1179648 | tf_op jit(solution)/shard_map/all_to_all | solution.py:68
  570.0 0.9 copy.70
  (54 shorter events, 5.7 us)
Async XLA Ops:
  0.0 29.7 %copy-start.2 = (s32[6,16]{1,0:T(8,128)S(1)}, s32[6,16]{1,0:T(8,128)}, u32[]{:S(2)}) copy-start(s32[6,16]{1,0:T(8,128)} %param.10) | copy-start | bytes 1156
  0.0 83.3 %copy-start.1 = (bf16[96,3072]{1,0:T(8,128)(2,1)S(1)}, bf16[96,3072]{1,0:T(8,128)(2,1)}, u32[]{:S(2)}) copy-start(bf16[96,3072]{1,0:T(8,128)(2,1)} %param.7) | copy-start | bytes 1769476
  2.0 24.1 %all-to-all-start = ((bf16[96,8,384]{2,0,1:T(8,128)(2,1)}), bf16[96,8,384]{2,0,1:T(8,128)(2,1)S(1)}, u32[]{:S(2)}, u32[]{:S(2)}) async-start(bf16[96,8,384]{2,0,1:T(8,128)(2,1)} %bitcast.73), calls=%async_computation | async-start | bytes 1179648 | tf_op jit(solution)/shard_map/all_to_all | solution.py:17
  26.1 58.1 %all-to-all-start.3 = ((bf16[96,8,384]{2,0,1:T(8,128)(2,1)}), bf16[96,8,384]{2,0,1:T(8,128)(2,1)S(1)}, u32[]{:S(2)}, u32[]{:S(2)}) async-start(bf16[96,8,384]{2,0,1:T(8,128)(2,1)} %bitcast.71), calls=%async_computation.3 | async-start | bytes 1179648 | tf_op jit(solution)/shard_map/all_to_all | solution.py:16
  84.2 26.2 %all-to-all-start.2 = ((bf16[96,8,384]{2,0,1:T(8,128)(2,1)}), bf16[96,8,384]{2,0,1:T(8,128)(2,1)S(1)}, u32[]{:S(2)}, u32[]{:S(2)}) async-start(bf16[96,8,384]{2,0,1:T(8,128)(2,1)} %bitcast.72), calls=%async_computation.2 | async-start | bytes 1179648 | tf_op jit(solution)/shard_map/all_to_all | solution.py:15
  110.4 146.7 %all-to-all-start.1 = ((bf16[64,128,384]{2,1,0:T(8,128)(2,1)}), bf16[64,128,384]{2,1,0:T(8,128)(2,1)}, u32[]{:S(2)}, u32[]{:S(2)}) async-start(bf16[64,128,384]{2,1,0:T(8,128)(2,1)} %gather_fusion.3), calls=%async_computation.1 | async-start | bytes 12582912 | tf_op jit(solution)/shard_map/all_to_all | solution.py:35
  257.1 146.8 %all-to-all-start.4 = ((bf16[64,128,384]{2,1,0:T(8,128)(2,1)}), bf16[64,128,384]{2,1,0:T(8,128)(2,1)}, u32[]{:S(2)}, u32[]{:S(2)}) async-start(bf16[64,128,384]{2,1,0:T(8,128)(2,1)} %gather_fusion.4), calls=%async_computation.4 | async-start | bytes 12582912 | tf_op jit(solution)/shard_map/all_to_all | solution.py:34
  412.5 13.1 %copy-start = (s32[384]{0:T(512)S(1)}, s32[384]{0:T(512)}, u32[]{:S(2)}) copy-start(s32[384]{0:T(512)} %param.11) | copy-start | bytes 4612
where the time goes:
time: 573 us; the launch traced here: 571 us
  waiting for transfers between devices  284 us (50%)
  local copies, waits for them, and re-layouts  146 us (25%)
  blocking collectives  76.4 us (13%)
  starting transfers between devices  29.7 us (5%)
  matrix products  27.6 us (5%)
  other arithmetic  6.61 us (1%)
    all_to_all x1, waiting for transfers between devices, local(): lax.all_to_all(sent_values, 'blk', split_axis=0, concat_axis=0, tiled=True)  137 us
    all_to_all x1, waiting for transfers between devices, local(): lax.all_to_all(sent_keys, 'blk', split_axis=0, concat_axis=0, tiled=True)  118 us
    all_gather x1, blocking collectives, local(): all_lists = lax.all_gather(key_lists, 'blk', axis=0, tiled=True)  53.5 us
    gather x6, local copies, waits for them, and re-layouts, attend(): picked_values = got_values[slot_index]  41.7 us
    gather x12, local copies, waits for them, and re-layouts, attend(): picked_keys = got_keys[slot_index]  36.9 us
    unnamed x9, local copies, waits for them, and re-layouts  27.2 us
    all_to_all x1, blocking collectives, local(): lax.all_to_all(attended, 'uly', split_axis=0, concat_axis=1, tiled=True)  22.9 us
    dot_general x6, matrix products, attend(): jnp.einsum('hqst,sthd->qhd', weight, picked_values, preferred_element_typ...  18 us
  transfers between devices with their start and end apart: 5, of which 4 were waited for; matrix products, arithmetic and copies ran while one was open for 6% of the time, Pallas kernels for 0%

commit v1 on v0

v1 whole, which is shorter than its diff:
```python
import functools
import math

import jax
import jax.numpy as jnp
from jax import lax
from jax.experimental import pallas as pl
from jax.experimental.pallas import tpu as pltpu
from jax.sharding import PartitionSpec as P

HD = 128
TILE = 128
SEL = 16
LIVE = 96
X, Z, C, Y = 4, 8, 2, 8
HX = 3
HEADS = HX * Y
PART = 96
BLOCK = PART * Y
PER = BLOCK // TILE
CROWS = BLOCK // 2
KEYS = SEL * LIVE
GROUPS = LIVE // 32
HALF = X // 2 * PER * GROUPS
HOPS = ((4, 3), (3, 4))
MESH = pl.DeviceIdType.MESH
C2 = math.log2(math.e) / math.sqrt(HD)


def kernel(
    q_ref, k_ref, v_ref, list_ref, fill_ref, out_ref,
    kpack, vpack, kbuf, vbuf, qbuf, obuf, gath, probs, totals, lsend, lrecv, lists,
    p1_send, p1_recv, q_recv, ring_send, ring_recv, sib_send, sib_recv, l_send, l_recv, l_copy, o_send, o_recv,
):
    blk, y = lax.axis_index("blk"), lax.axis_index("uly")
    x, z, c = blk // (Z * C), (blk // C) % Z, blk % C
    plane = z * C + c
    r, a = y % 4, y // 4

    def blk_at(xx):
        return xx * (Z * C) + plane

    barrier = pltpu.get_barrier_semaphore()
    me = x * Y + y

    def greet(j, _):
        p = (me + j) % (X * Y)
        pl.semaphore_signal(barrier, inc=1, device_id=(blk_at(p // Y), p % Y), device_id_type=MESH)
        return 0

    lax.fori_loop(1, X * Y, greet, 0)
    right = (x * (Z * C) + ((z + 1) % Z) * C + c, y)
    left = (x * (Z * C) + ((z + Z - 1) % Z) * C + c, y)
    other = (x * (Z * C) + z * C + (1 - c), y)
    for d in (right, left, other):
        pl.semaphore_signal(barrier, inc=1, device_id=d, device_id_type=MESH)

    first = pl.multiple_of(jnp.where(r == 1, 32, 0), 32)
    second = pl.multiple_of(jnp.where((r == 1) | (r == 2), 64, 32), 32)
    for src, dst in ((k_ref, kpack), (v_ref, vpack)):
        for h in range(HEADS):
            cols = slice(h * HD, (h + 1) * HD)
            dst[h, 0] = src[pl.ds(first, 32), cols]
            dst[h, 1] = src[pl.ds(second, 32), cols]
            dst[h, 2] = src[64:96, cols]
    lsend[...] = jnp.zeros_like(lsend)
    tile = list_ref[...]
    owner = (tile * 10923) >> 16
    place = ((owner & (Z * C - 1)) * X + (owner >> 4)) * PER + tile - owner * PER
    lsend[0:PER, 0:SEL] = tile
    lsend[8 : 8 + PER, 0:SEL] = place * GROUPS

    pl.semaphore_wait(barrier, X * Y - 1 + 3)

    off = ((plane * X + x) * PER + 3 * a) * GROUPS + jnp.where(r == 0, 0, 1 + 2 * r)
    half = x // 2

    def to_heads(i, act):
        yh, xh = (y + 4 + i // HX) % Y, (x + i) % HX
        act(yh * HX + xh, (blk_at(xh), yh), (xh == x) & (yh == y))

    def rows_copy(t, i, rows, wait):
        pack, buf = ((kpack, kbuf), (vpack, vbuf))[t]

        def act(h, device, own):
            src = pack.at[h, pl.ds(0, rows)]
            dst = buf.at[pl.ds(off, rows)]

            @pl.when(jnp.logical_not(own))
            def _():
                copy = pltpu.make_async_remote_copy(
                    src_ref=src, dst_ref=dst, send_sem=p1_send.at[t, i], recv_sem=p1_recv.at[t, half],
                    device_id=device, device_id_type=MESH,
                )
                copy.wait_send() if wait else copy.start()

            if not wait:

                @pl.when(own)
                def _():
                    pltpu.make_async_copy(src, dst, p1_recv.at[t, half]).start()

        to_heads(i, act)

    def q_copy(i, wait):
        def act(h, device, own):
            src = q_ref.at[:, pl.ds(pl.multiple_of(h * HD, HD), HD)]
            dst = qbuf.at[x, pl.ds(pl.multiple_of(y * PART, 32), PART)]

            @pl.when(jnp.logical_not(own))
            def _():
                copy = pltpu.make_async_remote_copy(
                    src_ref=src, dst_ref=dst, send_sem=p1_send.at[2, i], recv_sem=q_recv.at[0],
                    device_id=device, device_id_type=MESH,
                )
                copy.wait_send() if wait else copy.start()

            if not wait:

                @pl.when(own)
                def _():
                    pltpu.make_async_copy(src, dst, q_recv.at[0]).start()

        to_heads(i, act)

    def each_owner(body):
        def step(i, _):
            body(i)
            return 0

        lax.fori_loop(0, HEADS, step, 0)

    def all_rows(t, wait):
        @pl.when(r == 0)
        def _():
            each_owner(lambda i: rows_copy(t, i, 3, wait))

        @pl.when(r != 0)
        def _():
            each_owner(lambda i: rows_copy(t, i, 2, wait))

    all_rows(0, False)
    all_rows(1, False)
    each_owner(lambda i: q_copy(i, False))

    def list_copy(j):
        return pltpu.make_async_remote_copy(
            src_ref=lsend, dst_ref=lrecv.at[x], send_sem=l_send.at[j - 1], recv_sem=l_recv.at[j - 1],
            device_id=(blk_at((x + j) % X), y), device_id_type=MESH,
        )

    def list_arrival(j):
        return pltpu.make_async_remote_copy(
            src_ref=lsend, dst_ref=lrecv.at[(x + X - j) % X], send_sem=l_send.at[j - 1], recv_sem=l_recv.at[j - 1],
            device_id=(blk_at((x + j) % X), y), device_id_type=MESH,
        )

    for j in range(1, X):
        list_copy(j).start()

    def o_copy(n, xq, u, wait):
        src = obuf.at[xq, pl.ds(pl.multiple_of(u * PART, 32), PART)]
        dst = out_ref.at[:, pl.ds(pl.multiple_of((y * HX + x) * HD, HD), HD)]
        own = (xq == x) & (u == y)

        @pl.when(jnp.logical_not(own))
        def _():
            copy = pltpu.make_async_remote_copy(
                src_ref=src, dst_ref=dst, send_sem=o_send.at[n], recv_sem=o_recv.at[0],
                device_id=(blk_at(xq), u), device_id_type=MESH,
            )
            copy.wait_send() if wait else copy.start()

        if not wait:

            @pl.when(own)
            def _():
                pltpu.make_async_copy(src, dst, o_recv.at[0]).start()

    @pl.when(x < HX)
    def _():
        bufs = (kbuf, vbuf)

        def piece(t, zz, core, h):
            return bufs[t].at[pl.ds(((zz * C + core) * 2 + h) * HALF, HALF)]

        def ring(t, way, h, k):
            origin = (z + (Z - (k - 1) if way == 0 else k - 1)) % Z
            part = piece(t, origin, c, h)
            return pltpu.make_async_remote_copy(
                src_ref=part, dst_ref=part, send_sem=ring_send.at[t, way, h, k - 1], recv_sem=ring_recv.at[t, way, h, k - 1],
                device_id=(right, left)[way], device_id_type=MESH,
            )

        def ring_arrival(t, way, h, k):
            origin = (z + (Z - k if way == 0 else k)) % Z
            part = piece(t, origin, c, h)
            return pltpu.make_async_remote_copy(
                src_ref=part, dst_ref=part, send_sem=ring_send.at[t, way, h, k - 1], recv_sem=ring_recv.at[t, way, h, k - 1],
                device_id=(right, left)[way], device_id_type=MESH,
            )

        def sibling(t, shift, h, core):
            part = piece(t, (z + shift) % Z, core, h)
            return pltpu.make_async_remote_copy(
                src_ref=part, dst_ref=part, send_sem=sib_send.at[t, shift, h], recv_sem=sib_recv.at[t, shift, h],
                device_id=other, device_id_type=MESH,
            )

        def own_part(t, h):
            part = piece(t, z, c, h)
            pltpu.make_async_copy(part, part, p1_recv.at[t, h]).wait()
            for way in (0, 1):
                ring(t, way, h, 1).start()
            sibling(t, 0, h, c).start()

        def pass_on(t, h, k):
            for way in (0, 1):
                if k > HOPS[h][way]:
                    continue
                ring_arrival(t, way, h, k).wait_recv()
                if k < HOPS[h][way]:
                    ring(t, way, h, k + 1).start()
                sibling(t, (Z - k) if way == 0 else k, h, c).start()

        def gather(i, buf):
            xq, s = (x + i // 2) % X, i % 2
            for j in range(SEL):
                at = lists[xq, 8 + 3 * s, j]
                gath[j * LIVE : (j + 1) * LIVE, :] = buf[pl.ds(at, GROUPS)].reshape(LIVE, HD)
            return xq, s

        def scores(i, _):
            xq, s = gather(i, kbuf)
            lane = lax.broadcasted_iota(jnp.int32, (1, KEYS), 1)
            end = jnp.zeros((1, KEYS), jnp.int32)
            for j in range(SEL):
                end = jnp.where(lane >= j * LIVE, fill_ref[lists[xq, 3 * s, j]] + j * LIVE, end)
            bias = jnp.where(lane < end, 0.0, -1e30)
            for n in range(3):
                rows = pl.ds(pl.multiple_of(s * CROWS + n * TILE, TILE), TILE)
                sc = lax.dot_general(
                    qbuf[xq, rows, :], gath[...], (((1,), (1,)), ((), ())), preferred_element_type=jnp.float32
                )
                sc = sc + bias
                peak = jnp.max(sc, axis=1, keepdims=True)
                w = jnp.exp2((sc - peak) * C2)
                totals[i, n * TILE : (n + 1) * TILE, :] = jnp.sum(w, axis=1, keepdims=True)
                probs[i, n * TILE : (n + 1) * TILE, :] = w.astype(jnp.bfloat16)
            return 0

        def mix(i, _):
            xq, s = gather(i, vbuf)
            for n in range(3):
                rows = pl.ds(pl.multiple_of(s * CROWS + n * TILE, TILE), TILE)
                o = jnp.dot(probs[i, n * TILE : (n + 1) * TILE, :], gath[...], preferred_element_type=jnp.float32)
                obuf[xq, rows, :] = (o / totals[i, n * TILE : (n + 1) * TILE, :]).astype(jnp.bfloat16)
            for w in range(4):
                o_copy(4 * i + w, xq, 4 * s + w, False)
            return 0

        for h in (0, 1):
            own_part(0, h)
        for k in range(1, 4):
            for h in (0, 1):
                pass_on(0, h, k)
        for h in (0, 1):
            own_part(1, h)
        for h in (0, 1):
            pass_on(0, h, 4)
        for j in range(1, X):
            list_arrival(j).wait_recv()
        lrecv[pl.ds(x, 1)] = lsend[...][None]
        copy = pltpu.make_async_copy(lrecv, lists, l_copy.at[0])
        copy.start()
        copy.wait()
        pltpu.make_async_copy(qbuf, qbuf, q_recv.at[0]).wait()
        for shift in range(Z):
            for h in (0, 1):
                sibling(0, shift, h, 1 - c).wait_recv()
        lax.fori_loop(0, 4, scores, 0)
        pass_on(1, 0, 1)
        lax.fori_loop(4, 6, scores, 0)
        pass_on(1, 1, 1)
        lax.fori_loop(6, 8, scores, 0)
        for k in range(2, 5):
            for h in (0, 1):
                pass_on(1, h, k)
        for shift in range(Z):
            for h in (0, 1):
                sibling(1, shift, h, 1 - c).wait_recv()
        lax.fori_loop(0, 8, mix, 0)

        for t in (0, 1):
            for h in (0, 1):
                for way in (0, 1):
                    for k in range(1, HOPS[h][way] + 1):
                        ring(t, way, h, k).wait_send()
                for shift in range(Z):
                    sibling(t, shift, h, c).wait_send()

        def sent(i, _):
            for w in range(4):
                o_copy(4 * i + w, (x + i // 2) % X, 4 * (i % 2) + w, True)
            return 0

        lax.fori_loop(0, 8, sent, 0)

    @pl.when(x == HX)
    def _():
        for j in range(1, X):
            list_arrival(j).wait_recv()

    all_rows(0, True)
    all_rows(1, True)
    each_owner(lambda i: q_copy(i, True))
    for j in range(1, X):
        list_copy(j).wait_send()
    pltpu.make_async_copy(out_ref, out_ref, o_recv.at[0]).wait()


def local(queries, keys, values, key_lists, key_fill):
    bf = jnp.bfloat16
    vmem = pl.BlockSpec(memory_space=pltpu.VMEM)
    return pl.pallas_call(
        kernel,
        out_shape=jax.ShapeDtypeStruct(queries.shape, bf),
        in_specs=[vmem, vmem, vmem, vmem, pl.BlockSpec(memory_space=pltpu.SMEM)],
        out_specs=pl.BlockSpec(memory_space=pl.ANY),
        scratch_shapes=[
            pltpu.VMEM((HEADS, GROUPS, 32, HD), bf),
            pltpu.VMEM((HEADS, GROUPS, 32, HD), bf),
            pltpu.VMEM((Z * C * X * PER * GROUPS, 32, HD), bf),
            pltpu.VMEM((Z * C * X * PER * GROUPS, 32, HD), bf),
            pltpu.VMEM((X, BLOCK, HD), bf),
            pltpu.VMEM((X, BLOCK, HD), bf),
            pltpu.VMEM((KEYS, HD), bf),
            pltpu.VMEM((2 * X, CROWS, KEYS), bf),
            pltpu.VMEM((2 * X, CROWS, 1), jnp.float32),
            pltpu.VMEM((16, 128), jnp.int32),
            pltpu.VMEM((X, 16, 128), jnp.int32),
            pltpu.SMEM((X, 16, 128), jnp.int32),
            pltpu.SemaphoreType.DMA((3, HEADS)),
            pltpu.SemaphoreType.DMA((2, 2)),
            pltpu.SemaphoreType.DMA((1,)),
            pltpu.SemaphoreType.DMA((2, 2, 2, 4)),
            pltpu.SemaphoreType.DMA((2, 2, 2, 4)),
            pltpu.SemaphoreType.DMA((2, Z, 2)),
            pltpu.SemaphoreType.DMA((2, Z, 2)),
            pltpu.SemaphoreType.DMA((X - 1,)),
            pltpu.SemaphoreType.DMA((X - 1,)),
            pltpu.SemaphoreType.DMA((1,)),
            pltpu.SemaphoreType.DMA((X * Y,)),
            pltpu.SemaphoreType.DMA((1,)),
        ],
        compiler_params=pltpu.CompilerParams(
            collective_id=0, has_side_effects=True, vmem_limit_bytes=56 * 1024 * 1024
        ),
        cost_estimate=pl.CostEstimate(flops=5_000_000_000, bytes_accessed=4_000_000, transcendentals=4_800_000),
    )(queries, keys, values, key_lists, key_fill)


def solution(mesh):
    in_specs = (
        P(("blk", "uly"), None),
        P(("blk", "uly"), None),
        P(("blk", "uly"), None),
        P("blk", None),
        P(),
    )
    out_specs = P(("blk", "uly"), None)
    return jax.shard_map(local, mesh=mesh, in_specs=in_specs, out_specs=out_specs, check_vma=False)
```

time: 573 us -> 148 us (0.26)
  waiting for transfers between devices: 284 us -> 0 us
  Pallas kernels: 0 us -> 146 us
  local copies, waits for them, and re-layouts: 146 us -> 1.92 us
  blocking collectives: 76.4 us -> 0 us
  starting transfers between devices: 29.7 us -> 0 us
  matrix products: 27.6 us -> 0 us
  other arithmetic: 6.61 us -> 0 us
    all_to_all x5 -> x0, waiting for transfers between devices: 284 us -> none  [the longest x1 137 us: local(): lax.all_to_all(sent_values, 'blk', split_axis=0, concat_axis=0, tiled=True)]
    pallas_call x0 -> x1, Pallas kernels: none -> 146 us  [local(): pl.pallas_call(kernel, out_shape=jax.ShapeDtypeStruct(queries.shape, bf),...]
    gather x26 -> x0, local copies, waits for them, and re-layouts: 90.7 us -> none  [the longest x6 41.7 us: attend(): picked_values = got_values[slot_index]]
    all_gather x1 -> x0, blocking collectives: 53.5 us -> none  [local(): all_lists = lax.all_gather(key_lists, 'blk', axis=0, tiled=True)]
    all_to_all x5 -> x0, starting transfers between devices: 29.7 us -> none  [the longest x1 7.65 us: local(): lax.all_to_all(values, 'uly', split_axis=1, concat_axis=0, tiled=True)]
    unnamed x9 -> x1, local copies, waits for them, and re-layouts: 27.2 us -> 1.92 us
    all_to_all x6 -> x0, local copies, waits for them, and re-layouts: 23 us -> none  [the longest x1 8.62 us: local(): lax.all_to_all(sent_keys, 'blk', split_axis=0, concat_axis=0, tiled=True)]
    all_to_all x1 -> x0, blocking collectives: 22.9 us -> none  [local(): lax.all_to_all(attended, 'uly', split_axis=0, concat_axis=1, tiled=True)]
  transfers between devices with their start and end apart: 5 -> 0, of which waited for: 4 -> 0; matrix products, arithmetic and copies ran while one was open for 6% -> 0% of each run, Pallas kernels for 0% -> 0%
where the time goes in v1:
time: 148 us; the launch traced here: 147 us
  Pallas kernels  146 us (99%)
  local copies, waits for them, and re-layouts  1.92 us (1%)
    pallas_call x1, Pallas kernels, local(): pl.pallas_call(kernel, out_shape=jax.ShapeDtypeStruct(queries.shape, bf),...  146 us

profile of v1, /device:TPU:1, one launch (start us, length us, event | category | flops | bytes accessed | tf_op | source)
XLA Modules:
  0.0 147.5 jit_solution(1422093490902289279)
XLA Ops:
  0.0 145.6 %shard_map.55 = bf16[96,3072]{1,0:T(8,128)(2,1)} custom-call(bf16[96,3072]{1,0:T(8,128)(2,1)} %q_ref.1, bf16[96,3072]{1,0:T(8,128)(2,1)} %k_ref.1, bf16[96,3072]{1,0:T(8,128)(2,1)} %v_ref.1, s32[6,16]{1,0:T(8,128)} %list_ref.1, s32[384]{0:T(512)} %fill_ref.1), custom_call_target="tpu_custom_call" | custom-call | flops 5000000000 | bytes 4000000 | tf_op jit(solution)/shard_map/pallas_call | solution.py:325
  145.6 1.9 %copy.7 = bf16[96,3072]{1,0:T(8,128)(2,1)} copy(bf16[96,3072]{1,0:T(8,128)(2,1)} %shard_map.55) | data formatting | bytes 1179648

commit v2 on v1

v2 whole, which is shorter than its diff:
```python
import math

import jax
import jax.numpy as jnp
from jax import lax
from jax.experimental import pallas as pl
from jax.experimental.pallas import tpu as pltpu
from jax.sharding import PartitionSpec as P

HD = 128
TILE = 128
SEL = 16
LIVE = 96
X, Z, C, Y = 4, 8, 2, 8
HX = 3
HEADS = HX * Y
PART = 96
BLOCK = PART * Y
PER = BLOCK // TILE
CROWS = BLOCK // 2
KEYS = SEL * LIVE
GROUPS = LIVE // 32
SLOTS = 26
CHUNK = SLOTS * GROUPS
HALF = 10 * GROUPS
HALF3 = 6 * GROUPS
GUEST = 18 * GROUPS
LATE = 20 * GROUPS
HOPS = ((4, 3), (3, 4))
MESH = pl.DeviceIdType.MESH
C2 = math.log2(math.e) / math.sqrt(HD)


def kernel(
    q_ref, k_ref, v_ref, list_ref, fill_ref, out_ref,
    qin, kin, vin, kpack, vpack, kbuf, vbuf, qbuf, obuf, rbuf, gath, probs, totals, lsend, lrecv, lists,
    in_sem, p1_send, p1_recv, q_recv, ring_send, ring_recv, sib_send, sib_recv, dl_send, dl_recv, ds_send, ds_recv,
    l_send, l_recv, l_copy, o_send, o_recv, r_send, r_recv,
):
    blk, y = lax.axis_index("blk"), lax.axis_index("uly")
    x, z, c = blk // (Z * C), (blk // C) % Z, blk % C
    plane = z * C + c
    r, a = y % 4, y // 4

    reads = [
        pltpu.make_async_copy(src, dst, in_sem.at[n])
        for n, (src, dst) in enumerate(((k_ref, kin), (v_ref, vin), (q_ref, qin)))
    ]
    for copy in reads:
        copy.start()

    def blk_at(xx):
        return xx * (Z * C) + plane

    barrier = pltpu.get_barrier_semaphore()
    me = x * Y + y

    def greet(j, _):
        p = (me + j) % (X * Y)
        pl.semaphore_signal(barrier, inc=1, device_id=(blk_at(p // Y), p % Y), device_id_type=MESH)
        return 0

    lax.fori_loop(1, X * Y, greet, 0)
    right = (x * (Z * C) + ((z + 1) % Z) * C + c, y)
    left = (x * (Z * C) + ((z + Z - 1) % Z) * C + c, y)
    other = (x * (Z * C) + z * C + (1 - c), y)
    for d in (right, left, other):
        pl.semaphore_signal(barrier, inc=1, device_id=d, device_id_type=MESH)

    lsend[...] = jnp.zeros_like(lsend)
    tile = list_ref[...]
    owner = (tile * 10923) >> 16
    n = tile - owner * PER
    ox = owner >> 4
    start = (owner & (Z * C - 1)) * SLOTS
    edge = ox * PER + n + jnp.where(ox == 3, 2, 0)
    first = (n == 0) | (n == 3)
    outer = jnp.where(first, 20 + ox + jnp.where(n == 3, 1, 0), ox * 5 + n - 1 - jnp.where(n > 3, 1, 0))
    inner = jnp.where(ox == 1, 4, 14) + n
    middle = jnp.where((ox == 0) | (ox == 2), outer, inner)
    lsend[0:PER, 0:SEL] = tile
    lsend[8 : 8 + PER, 0:SEL] = (start + edge) * GROUPS
    lsend[16 : 16 + PER, 0:SEL] = (start + middle) * GROUPS

    piece0 = pl.multiple_of(jnp.where(r == 1, 32, 0), 32)
    piece1 = pl.multiple_of(jnp.where((r == 1) | (r == 2), 64, 32), 32)

    def pack(t):
        src, dst = ((kin, kpack), (vin, vpack))[t]
        reads[t].wait()
        for h in range(HEADS):
            cols = slice(h * HD, (h + 1) * HD)
            dst[h, 0] = src[pl.ds(piece0, 32), cols]
            dst[h, 1] = src[pl.ds(piece1, 32), cols]
            dst[h, 2] = src[64:96, cols]

    pack(0)
    pl.semaphore_wait(barrier, X * Y - 1 + 3)

    bufs = (kbuf, vbuf)

    def region(t, zz, core, at, count):
        return bufs[t].at[pl.ds((zz * C + core) * CHUNK + at, count)]

    off = jnp.where(r == 0, 0, 1 + 2 * r)
    wing = (x == 0) | (x == 2)
    i32 = jnp.int32

    def target(xh):
        if xh != 1:
            helped = x == 3
            xd = jnp.where(helped, 3, xh)
            at = jnp.where(helped, (PER if xh else 0), x * PER) * GROUPS + 9 * a + off
            half = jnp.where(helped, xh // 2, jnp.where((x == 2) | ((x == 1) & (a == 1) & (r != 0)), 1, 0))
            return xd, at, half
        guest = wing & (r == 0)
        xd = jnp.where(guest, x, 1)
        own = jnp.where(wing, 5 * x * GROUPS + 6 * a + off - 3, jnp.where(x == 1, 4, 14) * GROUPS + 9 * a + off)
        at = jnp.where(guest, GUEST + GROUPS * a, own)
        half = jnp.where(guest, 1, jnp.where(x >= 2, 1, 0))
        return xd, at, half

    targets = [target(xh) for xh in range(HX)]

    def rows_copy(t, i, rows, wait):
        yh = (y + 4 + i) % Y
        for xh, (xd, at, half) in enumerate(targets):
            own = (xd == x) & (yh == y)
            src = (kpack, vpack)[t].at[yh * HX + xh, pl.ds(0, rows)]
            dst = region(t, z, c, at, rows)

            @pl.when(jnp.logical_not(own))
            def _():
                copy = pltpu.make_async_remote_copy(
                    src_ref=src, dst_ref=dst, send_sem=p1_send.at[t, i * HX + xh], recv_sem=p1_recv.at[t, half],
                    device_id=(blk_at(xd), yh), device_id_type=MESH,
                )
                copy.wait_send() if wait else copy.start()

            if not wait:

                @pl.when(own)
                def _():
                    pltpu.make_async_copy(src, dst, p1_recv.at[t, half]).start()

    def q_copy(i, wait):
        yh = (y + 4 + i) % Y
        for xh in range(HX):
            own = (xh == x) & (yh == y)
            src = qin.at[:, pl.ds(pl.multiple_of((yh * HX + xh) * HD, HD), HD)]
            dst = qbuf.at[x, pl.ds(pl.multiple_of(y * PART, 32), PART)]

            @pl.when(jnp.logical_not(own))
            def _():
                copy = pltpu.make_async_remote_copy(
                    src_ref=src, dst_ref=dst, send_sem=p1_send.at[2, i * HX + xh], recv_sem=q_recv.at[0],
                    device_id=(blk_at(xh), yh), device_id_type=MESH,
                )
                copy.wait_send() if wait else copy.start()

            if not wait:

                @pl.when(own)
                def _():
                    pltpu.make_async_copy(src, dst, q_recv.at[0]).start()

    def each_y(body):
        def step(i, _):
            body(i)
            return 0

        lax.fori_loop(0, Y, step, 0)

    def all_rows(t, wait):
        @pl.when(r == 0)
        def _():
            each_y(lambda i: rows_copy(t, i, 3, wait))

        @pl.when(r != 0)
        def _():
            each_y(lambda i: rows_copy(t, i, 2, wait))

    all_rows(0, False)

    def list_copy(j):
        return pltpu.make_async_remote_copy(
            src_ref=lsend, dst_ref=lrecv.at[x], send_sem=l_send.at[j - 1], recv_sem=l_recv.at[j - 1],
            device_id=(blk_at((x + j) % X), y), device_id_type=MESH,
        )

    def list_arrival(j):
        return pltpu.make_async_remote_copy(
            src_ref=lsend, dst_ref=lrecv.at[(x + X - j) % X], send_sem=l_send.at[j - 1], recv_sem=l_recv.at[j - 1],
            device_id=(blk_at((x + j) % X), y), device_id_type=MESH,
        )

    for j in range(1, X):
        list_copy(j).start()

    def ring_copy(t, way, h, k, size, distance):
        origin = (z + (Z - distance if way == 0 else distance)) % Z
        part = region(t, origin, c, size * h, size)
        return pltpu.make_async_remote_copy(
            src_ref=part, dst_ref=part, send_sem=ring_send.at[t, way, h, k - 1], recv_sem=ring_recv.at[t, way, h, k - 1],
            device_id=(right, left)[way], device_id_type=MESH,
        )

    def sibling(t, shift, h, core):
        part = region(t, (z + shift) % Z, core, HALF * h, HALF)
        return pltpu.make_async_remote_copy(
            src_ref=part, dst_ref=part, send_sem=sib_send.at[t, shift, h], recv_sem=sib_recv.at[t, shift, h],
            device_id=other, device_id_type=MESH,
        )

    def guest(t, shift):
        origin = (z + shift) % Z
        return pltpu.make_async_remote_copy(
            src_ref=region(t, origin, c, GUEST, 2 * GROUPS), dst_ref=region(t, origin, c, LATE + GROUPS * x, 2 * GROUPS),
            send_sem=dl_send.at[t, shift, 0], recv_sem=dl_recv.at[t, shift, x // 2],
            device_id=(blk_at(1), y), device_id_type=MESH,
        )

    def hand_over(t, shift, h):
        origin = (z + shift) % Z
        return pltpu.make_async_remote_copy(
            src_ref=region(t, origin, c, HALF3 * h, HALF3), dst_ref=region(t, origin, c, LATE, HALF3),
            send_sem=dl_send.at[t, shift, h], recv_sem=dl_recv.at[t, shift, 0],
            device_id=(blk_at(2 * h), y), device_id_type=MESH,
        )

    def late_sibling(t, shift, core, tiles):
        part = region(t, (z + shift) % Z, core, LATE, tiles * GROUPS)
        return pltpu.make_async_remote_copy(
            src_ref=part, dst_ref=part, send_sem=ds_send.at[t, shift], recv_sem=ds_recv.at[t, shift],
            device_id=other, device_id_type=MESH,
        )

    def spread(t, shift, h):
        sibling(t, shift, h, c).start()
        if h == 1:

            @pl.when(x != 1)
            def _():
                guest(t, shift).start()

    def late(t, shift):
        @pl.when(x != 1)
        def _():
            part = region(t, (z + shift) % Z, c, LATE, HALF3)
            pltpu.make_async_copy(part, part, dl_recv.at[t, shift, 0]).wait()
            late_sibling(t, shift, c, 6).start()

        @pl.when(x == 1)
        def _():
            for n in (0, 1):
                part = region(t, (z + shift) % Z, c, LATE + 2 * GROUPS * n, 2 * GROUPS)
                pltpu.make_async_copy(part, part, dl_recv.at[t, shift, n]).wait()
            late_sibling(t, shift, c, 4).start()

    def own_part(t, h, helper):
        size = HALF3 if helper else HALF
        part = region(t, z, c, size * h, size)
        pltpu.make_async_copy(part, part, p1_recv.at[t, h]).wait()
        for way in (0, 1):
            ring_copy(t, way, h, 1, size, 0).start()
        hand_over(t, 0, h).start() if helper else spread(t, 0, h)

    def pass_on(t, h, k, helper):
        size = HALF3 if helper else HALF
        for way in (0, 1):
            if k > HOPS[h][way]:
                continue
            ring_copy(t, way, h, k, size, k).wait_recv()
            if k < HOPS[h][way]:
                ring_copy(t, way, h, k + 1, size, k).start()
            shift = (Z - k) if way == 0 else k
            hand_over(t, shift, h).start() if helper else spread(t, shift, h)

    def ring_sent(t, helper):
        size = HALF3 if helper else HALF
        for h in (0, 1):
            for way in (0, 1):
                for k in range(1, HOPS[h][way] + 1):
                    ring_copy(t, way, h, k, size, k - 1).wait_send()

    @pl.when(x < HX)
    def _():
        for h in (0, 1):
            own_part(0, h, False)

    @pl.when(x == HX)
    def _():
        for h in (0, 1):
            own_part(0, h, True)

    pack(1)
    all_rows(1, False)
    reads[2].wait()
    each_y(lambda i: q_copy(i, False))

    def o_copy(n, src, xq, u, xh, wait):
        dst = out_ref.at[:, pl.ds(pl.multiple_of((y * HX + xh) * HD, HD), HD)]
        own = (xq == x) & (u == y)

        @pl.when(jnp.logical_not(own))
        def _():
            copy = pltpu.make_async_remote_copy(
                src_ref=src, dst_ref=dst, send_sem=o_send.at[n], recv_sem=o_recv.at[0],
                device_id=(blk_at(xq), u), device_id_type=MESH,
            )
            copy.wait_send() if wait else copy.start()

        if not wait:

            @pl.when(own)
            def _():
                pltpu.make_async_copy(src, dst, o_recv.at[0]).start()

    @pl.when(x < HX)
    def _():
        place = jnp.where(x == 1, 16, 8)

        def cluster(i):
            return jnp.where(i < 2, 3, (x + i // 2) % HX), i % 2

        def gather(i, buf):
            xq, s = cluster(i)
            for j in range(SEL):
                at = lists[xq, place + 3 * s, j]
                gath[j * LIVE : (j + 1) * LIVE, :] = buf[pl.ds(at, GROUPS)].reshape(LIVE, HD)
            return xq, s

        def scores(i, _):
            xq, s = gather(i, kbuf)
            lane = lax.broadcasted_iota(jnp.int32, (1, KEYS), 1)
            end = jnp.zeros((1, KEYS), jnp.int32)
            for j in range(SEL):
                end = jnp.where(lane >= j * LIVE, fill_ref[lists[xq, 3 * s, j]] + j * LIVE, end)
            bias = jnp.where(lane < end, 0.0, -1e30)
            for n in range(3):
                rows = pl.ds(pl.multiple_of(s * CROWS + n * TILE, TILE), TILE)
                sc = lax.dot_general(
                    qbuf[xq, rows, :], gath[...], (((1,), (1,)), ((), ())), preferred_element_type=jnp.float32
                )
                sc = sc + bias
                peak = jnp.max(sc, axis=1, keepdims=True)
                w = jnp.exp2((sc - peak) * C2)
                totals[i, n * TILE : (n + 1) * TILE, :] = jnp.sum(w, axis=1, keepdims=True)
                probs[i, n * TILE : (n + 1) * TILE, :] = w.astype(jnp.bfloat16)
            return 0

        def block_piece(xq, u):
            return obuf.at[xq, pl.ds(pl.multiple_of(u * PART, 32), PART)]

        def relay(s):
            part = pl.ds(s * CROWS, CROWS)
            return pltpu.make_async_remote_copy(
                src_ref=obuf.at[HX, part], dst_ref=rbuf.at[x, part], send_sem=r_send.at[s], recv_sem=r_recv.at[x, s],
                device_id=(blk_at(HX), y), device_id_type=MESH,
            )

        def mix(i, _):
            xq, s = gather(i, vbuf)
            for n in range(3):
                rows = pl.ds(pl.multiple_of(s * CROWS + n * TILE, TILE), TILE)
                o = jnp.dot(probs[i, n * TILE : (n + 1) * TILE, :], gath[...], preferred_element_type=jnp.float32)
                obuf[xq, rows, :] = (o / totals[i, n * TILE : (n + 1) * TILE, :]).astype(jnp.bfloat16)
            return xq, s

        def mix_and_send(i, _):
            xq, s = mix(i, 0)
            for w in range(4):
                o_copy(4 * i + w, block_piece(xq, 4 * s + w), xq, 4 * s + w, x, False)
            return 0

        for k in range(1, 4):
            for h in (0, 1):
                pass_on(0, h, k, False)
            for shift in {k - 1, (Z - k + 1) % Z}:
                late(0, shift)
        for h in (0, 1):
            own_part(1, h, False)
        for h in (0, 1):
            pass_on(0, h, 4, False)
        for shift in (3, 5, 4):
            late(0, shift)
        for j in range(1, X):
            list_arrival(j).wait_recv()
        lrecv[pl.ds(x, 1)] = lsend[...][None]
        copy = pltpu.make_async_copy(lrecv, lists, l_copy.at[0])
        copy.start()
        copy.wait()
        pltpu.make_async_copy(qbuf, qbuf, q_recv.at[0]).wait()

        def from_sibling(t):
            for shift in range(Z):
                for h in (0, 1):
                    sibling(t, shift, h, 1 - c).wait_recv()

                @pl.when(x != 1)
                def _():
                    late_sibling(t, shift, 1 - c, 6).wait_recv()

                @pl.when(x == 1)
                def _():
                    late_sibling(t, shift, 1 - c, 4).wait_recv()

        from_sibling(0)
        lax.fori_loop(0, 4, scores, 0)
        pass_on(1, 0, 1, False)
        lax.fori_loop(4, 6, scores, 0)
        pass_on(1, 1, 1, False)
        lax.fori_loop(6, 8, scores, 0)
        late(1, 0)
        for k in range(2, 5):
            for h in (0, 1):
                pass_on(1, h, k, False)
            for shift in {k - 1, Z - k + 1}:
                late(1, shift)
        late(1, 4)
        from_sibling(1)
        for s in (0, 1):
            mix(s, 0)
            relay(s).start()
        lax.fori_loop(2, 8, mix_and_send, 0)

        for t in (0, 1):
            ring_sent(t, False)
            for shift in range(Z):
                for h in (0, 1):
                    sibling(t, shift, h, c).wait_send()

                @pl.when(x != 1)
                def _():
                    guest(t, shift).wait_send()
                    late_sibling(t, shift, c, 6).wait_send()

                @pl.when(x == 1)
                def _():
                    late_sibling(t, shift, c, 4).wait_send()

        for s in (0, 1):
            relay(s).wait_send()

        def sent(i, _):
            xq, s = cluster(i)
            for w in range(4):
                o_copy(4 * i + w, block_piece(xq, 4 * s + w), xq, 4 * s + w, x, True)
            return 0

        lax.fori_loop(2, 8, sent, 0)

    @pl.when(x == HX)
    def _():
        for k in range(1, 4):
            for h in (0, 1):
                pass_on(0, h, k, True)
        for h in (0, 1):
            own_part(1, h, True)
        for h in (0, 1):
            pass_on(0, h, 4, True)
        for k in range(1, 5):
            for h in (0, 1):
                pass_on(1, h, k, True)
        for j in range(1, X):
            list_arrival(j).wait_recv()
        for t in (0, 1):
            ring_sent(t, True)
            for shift in range(Z):
                for h in (0, 1):
                    hand_over(t, shift, h).wait_send()

        def column(wait):
            for s in (0, 1):
                for xh in range(HX):
                    if not wait:
                        part = rbuf.at[xh, pl.ds(s * CROWS, CROWS)]
                        pltpu.make_async_copy(part, part, r_recv.at[xh, s]).wait()
                    for w in range(4):
                        u = 4 * s + w
                        o_copy((s * HX + xh) * 4 + w, rbuf.at[xh, pl.ds(u * PART, PART)], x, u, xh, wait)

        column(False)
        column(True)

    all_rows(0, True)
    all_rows(1, True)
    each_y(lambda i: q_copy(i, True))
    for j in range(1, X):
        list_copy(j).wait_send()
    pltpu.make_async_copy(out_ref, out_ref, o_recv.at[0]).wait()


def local(queries, keys, values, key_lists, key_fill):
    bf = jnp.bfloat16
    anywhere = pl.BlockSpec(memory_space=pl.ANY)
    dma = pltpu.SemaphoreType.DMA
    return pl.pallas_call(
        kernel,
        out_shape=jax.ShapeDtypeStruct(queries.shape, bf),
        in_specs=[
            anywhere, anywhere, anywhere,
            pl.BlockSpec(memory_space=pltpu.VMEM), pl.BlockSpec(memory_space=pltpu.SMEM),
        ],
        out_specs=anywhere,
        scratch_shapes=[
            pltpu.VMEM((PART, HEADS * HD), bf),
            pltpu.VMEM((PART, HEADS * HD), bf),
            pltpu.VMEM((PART, HEADS * HD), bf),
            pltpu.VMEM((HEADS, GROUPS, 32, HD), bf),
            pltpu.VMEM((HEADS, GROUPS, 32, HD), bf),
            pltpu.VMEM((Z * C * CHUNK, 32, HD), bf),
            pltpu.VMEM((Z * C * CHUNK, 32, HD), bf),
            pltpu.VMEM((X, BLOCK, HD), bf),
            pltpu.VMEM((X, BLOCK, HD), bf),
            pltpu.VMEM((HX, BLOCK, HD), bf),
            pltpu.VMEM((KEYS, HD), bf),
            pltpu.VMEM((2 * X, CROWS, KEYS), bf),
            pltpu.VMEM((2 * X, CROWS, 1), jnp.float32),
            pltpu.VMEM((24, 128), jnp.int32),
            pltpu.VMEM((X, 24, 128), jnp.int32),
            pltpu.SMEM((X, 24, 128), jnp.int32),
            dma((3,)),
            dma((3, HEADS)),
            dma((2, 2)),
            dma((1,)),
            dma((2, 2, 2, 4)),
            dma((2, 2, 2, 4)),
            dma((2, Z, 2)),
            dma((2, Z, 2)),
            dma((2, Z, 2)),
            dma((2, Z, 2)),
            dma((2, Z)),
            dma((2, Z)),
            dma((X - 1,)),
            dma((X - 1,)),
            dma((1,)),
            dma((X * Y,)),
            dma((1,)),
            dma((2,)),
            dma((HX, 2)),
        ],
        compiler_params=pltpu.CompilerParams(
            collective_id=0, has_side_effects=True, vmem_limit_bytes=56 * 1024 * 1024
        ),
        cost_estimate=pl.CostEstimate(flops=5_000_000_000, bytes_accessed=4_000_000, transcendentals=4_800_000),
    )(queries, keys, values, key_lists, key_fill)


def solution(mesh):
    in_specs = (
        P(("blk", "uly"), None),
        P(("blk", "uly"), None),
        P(("blk", "uly"), None),
        P("blk", None),
        P(),
    )
    out_specs = P(("blk", "uly"), None)
    return jax.shard_map(local, mesh=mesh, in_specs=in_specs, out_specs=out_specs, check_vma=False)
```

time: 148 us -> 138 us (0.932)
  the two profiles are of different devices: /device:TPU:1 before, /device:TPU:55 now
where the time goes in v2:
time: 138 us
  Pallas kernels  136 us (99%)
  local copies, waits for them, and re-layouts  1.92 us (1%)
    pallas_call x1, Pallas kernels, local(): pl.pallas_call(kernel, out_shape=jax.ShapeDtypeStruct(queries.shape, bf),...  136 us

profile of v2, /device:TPU:55, one launch (start us, length us, event | category | flops | bytes accessed | tf_op | source)
XLA Modules:
  0.0 137.7 jit_solution(7292522137879518684)
XLA Ops:
  0.0 135.8 %shard_map.55 = bf16[96,3072]{1,0:T(8,128)(2,1)} custom-call(bf16[96,3072]{1,0:T(8,128)(2,1)} %q_ref.1, bf16[96,3072]{1,0:T(8,128)(2,1)} %k_ref.1, bf16[96,3072]{1,0:T(8,128)(2,1)} %v_ref.1, s32[6,16]{1,0:T(8,128)} %list_ref.1, s32[384]{0:T(512)} %fill_ref.1), custom_call_target="tpu_custom_call" | custom-call | flops 5000000000 | bytes 4000000 | tf_op jit(solution)/shard_map/pallas_call | solution.py:498
  135.8 1.9 %copy.7 = bf16[96,3072]{1,0:T(8,128)(2,1)} copy(bf16[96,3072]{1,0:T(8,128)(2,1)} %shard_map.55) | data formatting | bytes 1179648

commit v3 on v2

v3 whole, which is shorter than its diff:
```python
import math

import jax
import jax.numpy as jnp
from jax import lax
from jax.experimental import pallas as pl
from jax.experimental.pallas import tpu as pltpu
from jax.sharding import PartitionSpec as P

HD = 128
TILE = 128
SEL = 16
LIVE = 96
X, Z, C, Y = 4, 8, 2, 8
HX = 3
HEADS = HX * Y
PART = 96
BLOCK = PART * Y
PER = BLOCK // TILE
CROWS = BLOCK // 2
KEYS = SEL * LIVE
GROUPS = LIVE // 32
EDGE, MID, HELP = 0, 1, 2
BASE = (0, 34)
SIZE = {EDGE: (34, 26), MID: (32, 28), HELP: (20, 16)}
OWN = {EDGE: (30, 24), MID: (32, 28)}
LATE = 62
LATES = {EDGE: (10, 8), MID: (8, 4)}
CHUNK = 80
HOPS = ((4, 3), (3, 4))
MESH = pl.DeviceIdType.MESH
C2 = math.log2(math.e) / math.sqrt(HD)


def kernel(
    q_ref, k_ref, v_ref, list_ref, fill_ref, out_ref,
    qin, kin, vin, kpack, vpack, kbuf, vbuf, qbuf, obuf, rbuf, gath, probs, totals, lsend, lrecv, lists,
    in_sem, p1_send, p1_recv, q_recv, ring_send, ring_recv, sib_send, sib_recv, dl_send, dl_recv, ds_send, ds_recv,
    l_send, l_recv, l_copy, o_send, o_recv, r_send, r_recv,
):
    blk, y = lax.axis_index("blk"), lax.axis_index("uly")
    x, z, c = blk >> 4, (blk >> 1) & 7, blk & 1
    plane = blk & 15
    r, a = y & 3, y >> 2
    role_of = ((x & 1) == 0, x == 1, x == 3)

    def by_role(f, roles=(EDGE, MID, HELP)):
        for role in roles:
            pl.when(role_of[role])(lambda role=role: f(role))

    reads = [
        pltpu.make_async_copy(src, dst, in_sem.at[n])
        for n, (src, dst) in enumerate(((k_ref, kin), (v_ref, vin), (q_ref, qin)))
    ]
    for copy in reads:
        copy.start()

    def blk_at(xx):
        return (xx << 4) + plane

    barrier = pltpu.get_barrier_semaphore()
    right = ((blk & 49) + (((z + 1) & 7) << 1), y)
    left = ((blk & 49) + (((z + 7) & 7) << 1), y)
    other = (blk ^ 1, y)
    near = [(blk_at((x + i) & 3), (y + j) & 7) for j in range(Y) for i in range(X) if i or j]
    for d in (right, left, other, *near):
        pl.semaphore_signal(barrier, inc=1, device_id=d, device_id_type=MESH)

    piece0 = pl.multiple_of(jnp.where(r == 1, 32, 0), 32)
    piece1 = pl.multiple_of(jnp.where((r == 1) | (r == 2), 64, 32), 32)

    def pack(t):
        src, dst = ((kin, kpack), (vin, vpack))[t]
        reads[t].wait()
        for h in range(HEADS):
            cols = slice(h * HD, (h + 1) * HD)
            dst[h, 0] = src[pl.ds(piece0, 32), cols]
            dst[h, 1] = src[pl.ds(piece1, 32), cols]
            dst[h, 2] = src[64:96, cols]

    pack(0)
    pl.semaphore_wait(barrier, len(near) + 3)

    bufs = (kbuf, vbuf)

    def region(t, zz, core, at, count):
        return bufs[t].at[pl.ds((zz * C + core) * CHUNK + at, count)]

    off = jnp.where(r == 0, 0, 1 + r)
    wing = (x & 1) == 0

    def pick(values):
        out = values[-1]
        for n in range(len(values) - 1):
            out = jnp.where(x == n, values[n], out)
        return out

    def target(xh):
        if xh != 1:
            side = 1 if xh else 0
            return (
                jnp.where(x == 3, 3, xh),
                pick((0, 10, 20, 10 * side)) + 5 * a + off,
                BASE[1] + pick((0, 8, 16, 8 * side)) + 4 * a + r,
            )
        guest = wing & (r == 0)
        at0 = jnp.where(wing, 3 * a + r - 1, 5 * a + off) + pick((0, 6, 16, 22))
        at1 = jnp.where(wing, 3 * a + r - 1, 4 * a + r) + pick((0, 6, 14, 20))
        return (
            jnp.where(guest, x, 1),
            jnp.where(guest, OWN[EDGE][0] + 2 * a, at0),
            BASE[1] + jnp.where(guest, OWN[EDGE][1] + a, at1),
        )

    targets = [target(xh) for xh in range(HX)]
    second = jnp.where(r == 0, 2, 1)

    def rows_copy(t, h, i, rows, wait):
        yh = (y + 4 + i) & 7
        for xh, (xd, *at) in enumerate(targets):
            own = (xd == x) & (yh == y)
            src = (kpack, vpack)[t].at[yh * HX + xh, pl.ds(second if h else 0, rows)]
            dst = region(t, z, c, at[h], rows)

            @pl.when(jnp.logical_not(own))
            def _():
                copy = pltpu.make_async_remote_copy(
                    src_ref=src, dst_ref=dst, send_sem=p1_send.at[2 * t + h, i * HX + xh], recv_sem=p1_recv.at[t, h],
                    device_id=(blk_at(xd), yh), device_id_type=MESH,
                )
                copy.wait_send() if wait else copy.start()

            if not wait:

                @pl.when(own)
                def _():
                    pltpu.make_async_copy(src, dst, p1_recv.at[t, h]).start()

    def q_copy(i, wait):
        yh = (y + 4 + i) & 7
        for xh in range(HX):
            own = (xh == x) & (yh == y)
            src = qin.at[:, pl.ds(pl.multiple_of((yh * HX + xh) * HD, HD), HD)]
            dst = qbuf.at[x, pl.ds(pl.multiple_of(y * PART, 32), PART)]

            @pl.when(jnp.logical_not(own))
            def _():
                copy = pltpu.make_async_remote_copy(
                    src_ref=src, dst_ref=dst, send_sem=p1_send.at[4, i * HX + xh], recv_sem=q_recv.at[0],
                    device_id=(blk_at(xh), yh), device_id_type=MESH,
                )
                copy.wait_send() if wait else copy.start()

            if not wait:

                @pl.when(own)
                def _():
                    pltpu.make_async_copy(src, dst, q_recv.at[0]).start()

    def each_y(body):
        def step(i, _):
            body(i)
            return 0

        lax.fori_loop(0, Y, step, 0)

    def all_rows(t, h, wait):
        if h == 1:
            each_y(lambda i: rows_copy(t, h, i, 1, wait))
            return

        @pl.when(r == 0)
        def _():
            each_y(lambda i: rows_copy(t, h, i, 2, wait))

        @pl.when(r != 0)
        def _():
            each_y(lambda i: rows_copy(t, h, i, 1, wait))

    all_rows(0, 0, False)
    all_rows(0, 1, False)

    lsend[...] = jnp.zeros_like(lsend)
    tile = list_ref[...]
    owner = (tile * 10923) >> 16
    n = tile - owner * PER
    ox = owner >> 4
    later = jnp.where(n >= 3, 1, 0)
    q = n - 3 * later
    outer = (ox == 0) | (ox == 2)
    low = jnp.where(ox >= 2, 1, 0)
    edge0 = jnp.where(ox == 3, LATE + 5 * later, 5 * (2 * ox + later))
    edge1 = jnp.where(ox == 3, LATE + LATES[EDGE][0] + 4 * later, BASE[1] + 4 * (2 * ox + later))
    mid0 = jnp.where(outer, 16 * low + 3 * later - 2, 6 + 16 * low + 5 * later)
    mid1 = BASE[1] + jnp.where(outer, 14 * low + 3 * later - 1, 6 + 14 * low + 4 * later)
    away = outer & (q == 0)
    mid0 = jnp.where(away, LATE + 4 * low + 2 * later, mid0)
    mid1 = jnp.where(away, LATE + LATES[MID][0] + 2 * low + later, mid1)
    lsend[0:PER, 0:SEL] = tile
    start = (owner & (Z * C - 1)) * CHUNK
    for v, (b0, b1) in enumerate(((edge0, edge1), (mid0, mid1))):
        for g, (n0, n1, n2) in enumerate(((b0, b0 + 2, b1 + 2), (b0 + 1, b1 + 1, b0 + 4), (b1, b0 + 3, b1 + 3))):
            row = 8 * (1 + 3 * v + g)
            lsend[row : row + PER, 0:SEL] = start + jnp.where(q == 0, n0, jnp.where(q == 1, n1, n2))

    def list_copy(j):
        return pltpu.make_async_remote_copy(
            src_ref=lsend, dst_ref=lrecv.at[x], send_sem=l_send.at[j - 1], recv_sem=l_recv.at[j - 1],
            device_id=(blk_at((x + j) % X), y), device_id_type=MESH,
        )

    def list_arrival(j):
        return pltpu.make_async_remote_copy(
            src_ref=lsend, dst_ref=lrecv.at[(x + X - j) % X], send_sem=l_send.at[j - 1], recv_sem=l_recv.at[j - 1],
            device_id=(blk_at((x + j) % X), y), device_id_type=MESH,
        )

    def ring_copy(role, t, way, h, k, distance):
        origin = (z + (Z - distance if way == 0 else distance)) & 7
        part = region(t, origin, c, BASE[h], SIZE[role][h])
        return pltpu.make_async_remote_copy(
            src_ref=part, dst_ref=part, send_sem=ring_send.at[t, way, h, k - 1], recv_sem=ring_recv.at[t, way, h, k - 1],
            device_id=(right, left)[way], device_id_type=MESH,
        )

    def sibling(role, t, shift, h, core):
        part = region(t, (z + shift) & 7, core, BASE[h], OWN[role][h])
        return pltpu.make_async_remote_copy(
            src_ref=part, dst_ref=part, send_sem=sib_send.at[t, shift, h], recv_sem=sib_recv.at[t, shift, h],
            device_id=other, device_id_type=MESH,
        )

    def guest(t, shift, h):
        origin, count = (z + shift) & 7, (4, 2)[h]
        at = LATE + (2 * x, LATES[MID][0] + x)[h]
        return pltpu.make_async_remote_copy(
            src_ref=region(t, origin, c, BASE[h] + OWN[EDGE][h], count), dst_ref=region(t, origin, c, at, count),
            send_sem=dl_send.at[t, shift, h, 0], recv_sem=dl_recv.at[t, shift, h, x >> 1],
            device_id=(blk_at(1), y), device_id_type=MESH,
        )

    def hand_over(t, shift, h, side):
        origin, count = (z + shift) & 7, LATES[EDGE][h]
        return pltpu.make_async_remote_copy(
            src_ref=region(t, origin, c, BASE[h] + count * side, count),
            dst_ref=region(t, origin, c, LATE + (0, LATES[EDGE][0])[h], count),
            send_sem=dl_send.at[t, shift, h, side], recv_sem=dl_recv.at[t, shift, h, 0],
            device_id=(blk_at(2 * side), y), device_id_type=MESH,
        )

    def late_sibling(role, t, shift, core):
        part = region(t, (z + shift) & 7, core, LATE, sum(LATES[role]))
        return pltpu.make_async_remote_copy(
            src_ref=part, dst_ref=part, send_sem=ds_send.at[t, shift], recv_sem=ds_recv.at[t, shift],
            device_id=other, device_id_type=MESH,
        )

    def spread(role, t, shift, h):
        if role == HELP:
            for side in (0, 1):
                hand_over(t, shift, h, side).start()
            return
        sibling(role, t, shift, h, c).start()
        if role == EDGE:
            guest(t, shift, h).start()

    def late(role, t, shift):
        at = LATE
        for h in (0, 1):
            parts = (LATES[EDGE][h],) if role == EDGE else (LATES[MID][h] // 2,) * 2
            for n, count in enumerate(parts):
                part = region(t, (z + shift) & 7, c, at, count)
                pltpu.make_async_copy(part, part, dl_recv.at[t, shift, h, n]).wait()
                at += count
        late_sibling(role, t, shift, c).start()

    def own_part(role, t, h):
        part = region(t, z, c, BASE[h], SIZE[role][h])
        pltpu.make_async_copy(part, part, p1_recv.at[t, h]).wait()
        for way in (0, 1):
            ring_copy(role, t, way, h, 1, 0).start()
        spread(role, t, 0, h)

    def pass_on(role, t, h, k):
        for way in (0, 1):
            if k > HOPS[h][way]:
                continue
            ring_copy(role, t, way, h, k, k).wait_recv()
            if k < HOPS[h][way]:
                ring_copy(role, t, way, h, k + 1, k).start()
            spread(role, t, (Z - k) if way == 0 else k, h)

    def late_step(role, t, k):
        if role != HELP:
            for shift in sorted({k, (Z - k) % Z}):
                late(role, t, shift)

    def ring_sent(role, t):
        for h in (0, 1):
            for way in (0, 1):
                for k in range(1, HOPS[h][way] + 1):
                    ring_copy(role, t, way, h, k, k - 1).wait_send()
        for shift in range(Z):
            for h in (0, 1):
                if role == HELP:
                    for side in (0, 1):
                        hand_over(t, shift, h, side).wait_send()
                else:
                    sibling(role, t, shift, h, c).wait_send()
                if role == EDGE:
                    guest(t, shift, h).wait_send()
            if role != HELP:
                late_sibling(role, t, shift, c).wait_send()

    def from_sibling(role, t):
        for shift in range(Z):
            for h in (0, 1):
                sibling(role, t, shift, h, 1 - c).wait_recv()
            late_sibling(role, t, shift, 1 - c).wait_recv()

    for h in (0, 1):
        by_role(lambda role: own_part(role, 0, h))
    for j in range(1, X):
        list_copy(j).start()
    pack(1)
    all_rows(1, 0, False)
    by_role(lambda role: pass_on(role, 0, 0, 1))
    all_rows(1, 1, False)
    by_role(lambda role: pass_on(role, 0, 1, 1))
    reads[2].wait()
    each_y(lambda i: q_copy(i, False))

    def k_ring(role):
        late_step(role, 0, 0)
        for k in range(2, 4):
            for h in (0, 1):
                pass_on(role, 0, h, k)
            late_step(role, 0, k - 1)
        for h in (0, 1):
            own_part(role, 1, h)
        for h in (0, 1):
            pass_on(role, 0, h, 4)
        late_step(role, 0, 3)
        late_step(role, 0, 4)
        if role != HELP:
            from_sibling(role, 0)

    by_role(k_ring)

    def o_copy(n, src, xq, u, xh, wait):
        dst = out_ref.at[:, pl.ds(pl.multiple_of((y * HX + xh) * HD, HD), HD)]
        own = (xq == x) & (u == y)

        @pl.when(jnp.logical_not(own))
        def _():
            copy = pltpu.make_async_remote_copy(
                src_ref=src, dst_ref=dst, send_sem=o_send.at[n], recv_sem=o_recv.at[0],
                device_id=(blk_at(xq), u), device_id_type=MESH,
            )
            copy.wait_send() if wait else copy.start()

        if not wait:

            @pl.when(own)
            def _():
                pltpu.make_async_copy(src, dst, o_recv.at[0]).start()

    @pl.when(x < HX)
    def _():
        place = jnp.where(x == 1, 32, 8)
        both = (EDGE, MID)

        def cluster(i):
            return jnp.where(i < 2, 3, (x + (i >> 1)) % HX), i & 1

        def gather(i, buf):
            xq, s = cluster(i)
            for j in range(SEL):
                for g in range(GROUPS):
                    row = j * LIVE + g * 32
                    gath[row : row + 32, :] = buf[lists[xq, place + 8 * g + 3 * s, j]]
            return xq, s

        def scores(i, _):
            xq, s = gather(i, kbuf)
            lane = lax.broadcasted_iota(jnp.int32, (1, KEYS), 1)
            end = jnp.zeros((1, KEYS), jnp.int32)
            for j in range(SEL):
                end = jnp.where(lane >= j * LIVE, fill_ref[lists[xq, 3 * s, j]] + j * LIVE, end)
            bias = jnp.where(lane < end, 0.0, -1e30)
            for n in range(3):
                rows = pl.ds(pl.multiple_of(s * CROWS + n * TILE, TILE), TILE)
                sc = lax.dot_general(
                    qbuf[xq, rows, :], gath[...], (((1,), (1,)), ((), ())), preferred_element_type=jnp.float32
                )
                sc = sc + bias
                peak = jnp.max(sc, axis=1, keepdims=True)
                w = jnp.exp2((sc - peak) * C2)
                totals[i, n * TILE : (n + 1) * TILE, :] = jnp.sum(w, axis=1, keepdims=True)
                probs[i, n * TILE : (n + 1) * TILE, :] = w.astype(jnp.bfloat16)
            return 0

        def block_piece(xq, u):
            return obuf.at[xq, pl.ds(pl.multiple_of(u * PART, 32), PART)]

        relay = pltpu.make_async_remote_copy(
            src_ref=obuf.at[HX, pl.ds(0, CROWS)], dst_ref=rbuf.at[x], send_sem=r_send.at[0], recv_sem=r_recv.at[x],
            device_id=(blk_at(HX), y), device_id_type=MESH,
        )

        def mix(i, _):
            xq, s = gather(i, vbuf)
            for n in range(3):
                rows = pl.ds(pl.multiple_of(s * CROWS + n * TILE, TILE), TILE)
                o = jnp.dot(probs[i, n * TILE : (n + 1) * TILE, :], gath[...], preferred_element_type=jnp.float32)
                obuf[xq, rows, :] = (o / totals[i, n * TILE : (n + 1) * TILE, :]).astype(jnp.bfloat16)
            return xq, s

        def mix_and_send(i, _):
            xq, s = mix(i, 0)
            for w in range(4):
                o_copy(4 * i + w, block_piece(xq, 4 * s + w), xq, 4 * s + w, x, False)
            return 0

        for j in range(1, X):
            list_arrival(j).wait_recv()
        lrecv[pl.ds(x, 1)] = lsend[...][None]
        copy = pltpu.make_async_copy(lrecv, lists, l_copy.at[0])
        copy.start()
        copy.wait()
        pltpu.make_async_copy(qbuf, qbuf, q_recv.at[0]).wait()

        lax.fori_loop(0, 4, scores, 0)
        by_role(lambda role: pass_on(role, 1, 0, 1), both)
        lax.fori_loop(4, 6, scores, 0)
        by_role(lambda role: pass_on(role, 1, 1, 1), both)
        lax.fori_loop(6, 8, scores, 0)

        def v_ring(role):
            late_step(role, 1, 0)
            for k in range(2, 5):
                for h in (0, 1):
                    pass_on(role, 1, h, k)
                late_step(role, 1, k - 1)
            late_step(role, 1, 4)
            from_sibling(role, 1)

        by_role(v_ring, both)
        mix(0, 0)
        relay.start()
        lax.fori_loop(1, 8, mix_and_send, 0)

        def done(role):
            for t in (0, 1):
                ring_sent(role, t)

        by_role(done, both)
        relay.wait_send()

        def sent(i, _):
            xq, s = cluster(i)
            for w in range(4):
                o_copy(4 * i + w, block_piece(xq, 4 * s + w), xq, 4 * s + w, x, True)
            return 0

        lax.fori_loop(1, 8, sent, 0)

    @pl.when(x == HX)
    def _():
        for k in range(1, 5):
            for h in (0, 1):
                pass_on(HELP, 1, h, k)
        for j in range(1, X):
            list_arrival(j).wait_recv()
        for t in (0, 1):
            ring_sent(HELP, t)

        def column(wait):
            for xh in range(HX):
                if not wait:
                    pltpu.make_async_copy(rbuf.at[xh], rbuf.at[xh], r_recv.at[xh]).wait()
                for w in range(4):
                    o_copy(4 * xh + w, rbuf.at[xh, pl.ds(w * PART, PART)], x, w, xh, wait)

        column(False)
        column(True)

    for t in (0, 1):
        for h in (0, 1):
            all_rows(t, h, True)
    each_y(lambda i: q_copy(i, True))
    for j in range(1, X):
        list_copy(j).wait_send()
    pltpu.make_async_copy(out_ref, out_ref, o_recv.at[0]).wait()


def local(queries, keys, values, key_lists, key_fill):
    bf = jnp.bfloat16
    anywhere = pl.BlockSpec(memory_space=pl.ANY)
    dma = pltpu.SemaphoreType.DMA
    return pl.pallas_call(
        kernel,
        out_shape=jax.ShapeDtypeStruct(queries.shape, bf),
        in_specs=[
            anywhere, anywhere, anywhere,
            pl.BlockSpec(memory_space=pltpu.VMEM), pl.BlockSpec(memory_space=pltpu.SMEM),
        ],
        out_specs=anywhere,
        scratch_shapes=[
            pltpu.VMEM((PART, HEADS * HD), bf),
            pltpu.VMEM((PART, HEADS * HD), bf),
            pltpu.VMEM((PART, HEADS * HD), bf),
            pltpu.VMEM((HEADS, GROUPS, 32, HD), bf),
            pltpu.VMEM((HEADS, GROUPS, 32, HD), bf),
            pltpu.VMEM((Z * C * CHUNK, 32, HD), bf),
            pltpu.VMEM((Z * C * CHUNK, 32, HD), bf),
            pltpu.VMEM((X, BLOCK, HD), bf),
            pltpu.VMEM((X, BLOCK, HD), bf),
            pltpu.VMEM((HX, CROWS, HD), bf),
            pltpu.VMEM((KEYS, HD), bf),
            pltpu.VMEM((2 * X, CROWS, KEYS), bf),
            pltpu.VMEM((2 * X, CROWS, 1), jnp.float32),
            pltpu.VMEM((56, 128), jnp.int32),
            pltpu.VMEM((X, 56, 128), jnp.int32),
            pltpu.SMEM((X, 56, 128), jnp.int32),
            dma((3,)),
            dma((5, HEADS)),
            dma((2, 2)),
            dma((1,)),
            dma((2, 2, 2, 4)),
            dma((2, 2, 2, 4)),
            dma((2, Z, 2)),
            dma((2, Z, 2)),
            dma((2, Z, 2, 2)),
            dma((2, Z, 2, 2)),
            dma((2, Z)),
            dma((2, Z)),
            dma((X - 1,)),
            dma((X - 1,)),
            dma((1,)),
            dma((X * Y,)),
            dma((1,)),
            dma((1,)),
            dma((HX,)),
        ],
        compiler_params=pltpu.CompilerParams(
            collective_id=0, has_side_effects=True, vmem_limit_bytes=56 * 1024 * 1024
        ),
        cost_estimate=pl.CostEstimate(flops=5_000_000_000, bytes_accessed=4_000_000, transcendentals=4_800_000),
    )(queries, keys, values, key_lists, key_fill)


def solution(mesh):
    in_specs = (
        P(("blk", "uly"), None),
        P(("blk", "uly"), None),
        P(("blk", "uly"), None),
        P("blk", None),
        P(),
    )
    out_specs = P(("blk", "uly"), None)
    return jax.shard_map(local, mesh=mesh, in_specs=in_specs, out_specs=out_specs, check_vma=False)
```

time: 138 us -> 145 us (1.051)
  the two profiles are of different devices: /device:TPU:55 before, /device:TPU:23 now
where the time goes in v3:
time: 145 us
  Pallas kernels  143 us (99%)
  local copies, waits for them, and re-layouts  1.92 us (1%)
    pallas_call x1, Pallas kernels, local(): pl.pallas_call(kernel, out_shape=jax.ShapeDtypeStruct(queries.shape, bf),...  143 us

profile of v3, /device:TPU:23, one launch (start us, length us, event | category | flops | bytes accessed | tf_op | source)
XLA Modules:
  0.0 144.6 jit_solution(17361925612938355179)
XLA Ops:
  0.0 142.6 %shard_map.55 = bf16[96,3072]{1,0:T(8,128)(2,1)} custom-call(bf16[96,3072]{1,0:T(8,128)(2,1)} %q_ref.1, bf16[96,3072]{1,0:T(8,128)(2,1)} %k_ref.1, bf16[96,3072]{1,0:T(8,128)(2,1)} %v_ref.1, s32[6,16]{1,0:T(8,128)} %list_ref.1, s32[384]{0:T(512)} %fill_ref.1), custom_call_target="tpu_custom_call" | custom-call | flops 5000000000 | bytes 4000000 | tf_op jit(solution)/shard_map/pallas_call | solution.py:501
  142.7 1.9 %copy.7 = bf16[96,3072]{1,0:T(8,128)(2,1)} copy(bf16[96,3072]{1,0:T(8,128)(2,1)} %shard_map.55) | data formatting | bytes 1179648

commit v4 on v2

v4 whole, which is shorter than its diff:
```python
import math

import jax
import jax.numpy as jnp
from jax import lax
from jax.experimental import pallas as pl
from jax.experimental.pallas import tpu as pltpu
from jax.sharding import PartitionSpec as P

HD = 128
TILE = 128
SEL = 16
LIVE = 96
X, Z, C, Y = 4, 8, 2, 8
HX = 3
HEADS = HX * Y
PART = 96
BLOCK = PART * Y
PER = BLOCK // TILE
CROWS = BLOCK // 2
KEYS = SEL * LIVE
GROUPS = LIVE // 32
SLOTS = 26
CHUNK = SLOTS * GROUPS
LATE = 20 * GROUPS
GUEST = 18 * GROUPS
EDGE, MID, HELP = 0, 1, 2
PARTS = {EDGE: ((2, 54, 6), (0, 0, 30), (1, 30, 24)), MID: ((0, 0, 30), (1, 30, 30)), HELP: ((0, 0, 18), (1, 18, 18))}
HOPS = ((4, 3), (3, 4), (3, 4))
MESH = pl.DeviceIdType.MESH
C2 = math.log2(math.e) / math.sqrt(HD)


def kernel(
    q_ref, k_ref, v_ref, list_ref, fill_ref, out_ref,
    qin, kin, vin, kpack, vpack, kbuf, vbuf, qbuf, obuf, gath, probs, totals, lsend, lrecv, lists,
    in_sem, p1_send, p1_recv, q_recv, ring_send, ring_recv, sib_send, sib_recv, dl_send, dl_recv, ds_send, ds_recv,
    l_send, l_recv, l_copy, o_send, o_recv,
):
    blk, y = lax.axis_index("blk"), lax.axis_index("uly")
    x, z, c = blk >> 4, (blk >> 1) & 7, blk & 1
    plane = blk & 15
    r, a = y & 3, y >> 2
    role_of = ((x & 1) == 0, x == 1, x == 3)

    def by_role(f, roles=(EDGE, MID, HELP)):
        for role in roles:
            pl.when(role_of[role])(lambda role=role: f(role))

    reads = [
        pltpu.make_async_copy(src, dst, in_sem.at[n])
        for n, (src, dst) in enumerate(((k_ref, kin), (v_ref, vin), (q_ref, qin)))
    ]
    for copy in reads:
        copy.start()

    def blk_at(xx):
        return (xx << 4) + plane

    barrier = pltpu.get_barrier_semaphore()
    right = ((blk & 49) + (((z + 1) & 7) << 1), y)
    left = ((blk & 49) + (((z + 7) & 7) << 1), y)
    other = (blk ^ 1, y)
    near = [(blk_at((x + i) & 3), (y + j) & 7) for j in range(Y) for i in range(X) if i or j]
    for d in (right, left, other, *near):
        pl.semaphore_signal(barrier, inc=1, device_id=d, device_id_type=MESH)

    lsend[...] = jnp.zeros_like(lsend)
    tile = list_ref[...]
    owner = (tile * 10923) >> 16
    n = tile - owner * PER
    ox = owner >> 4
    start = (owner & (Z * C - 1)) * SLOTS
    edge = ox * PER + n + jnp.where(ox == 3, 2, 0)
    first = (n == 0) | (n == 3)
    outer = jnp.where(first, 20 + ox + jnp.where(n == 3, 1, 0), ox * 5 + n - 1 - jnp.where(n > 3, 1, 0))
    inner = jnp.where(ox == 1, 4, 14) + n
    middle = jnp.where((ox == 0) | (ox == 2), outer, inner)
    lsend[0:PER, 0:SEL] = tile
    lsend[8 : 8 + PER, 0:SEL] = (start + edge) * GROUPS
    lsend[16 : 16 + PER, 0:SEL] = (start + middle) * GROUPS

    piece0 = pl.multiple_of(jnp.where(r == 1, 32, 0), 32)
    piece1 = pl.multiple_of(jnp.where((r == 1) | (r == 2), 64, 32), 32)

    def pack(t):
        src, dst = ((kin, kpack), (vin, vpack))[t]
        reads[t].wait()
        for h in range(HEADS):
            cols = slice(h * HD, (h + 1) * HD)
            dst[h, 0] = src[pl.ds(piece0, 32), cols]
            dst[h, 1] = src[pl.ds(piece1, 32), cols]
            dst[h, 2] = src[64:96, cols]

    pack(0)
    pl.semaphore_wait(barrier, len(near) + 3)

    bufs = (kbuf, vbuf)

    def region(t, zz, core, at, count):
        return bufs[t].at[pl.ds((zz * C + core) * CHUNK + at, count)]

    off = jnp.where(r == 0, 0, 1 + 2 * r)
    wing = (x == 0) | (x == 2)
    i32 = jnp.int32

    def target(xh):
        if xh != 1:
            helped = x == 3
            xd = jnp.where(helped, 3, xh)
            at = jnp.where(helped, (PER if xh else 0), x * PER) * GROUPS + 9 * a + off
            half = jnp.where(helped, xh // 2, jnp.where((x == 2) | ((x == 1) & (a == 1) & (r != 0)), 1, 0))
            return xd, at, half
        guest = wing & (r == 0)
        xd = jnp.where(guest, x, 1)
        own = jnp.where(wing, 5 * x * GROUPS + 6 * a + off - 3, jnp.where(x == 1, 4, 14) * GROUPS + 9 * a + off)
        at = jnp.where(guest, GUEST + GROUPS * a, own)
        half = jnp.where(guest, 2, jnp.where(x >= 2, 1, 0))
        return xd, at, half

    targets = [target(xh) for xh in range(HX)]

    def rows_copy(t, i, rows, wait):
        yh = (y + 4 + i) & 7
        for xh, (xd, at, half) in enumerate(targets):
            own = (xd == x) & (yh == y)
            src = (kpack, vpack)[t].at[yh * HX + xh, pl.ds(0, rows)]
            dst = region(t, z, c, at, rows)

            @pl.when(jnp.logical_not(own))
            def _():
                copy = pltpu.make_async_remote_copy(
                    src_ref=src, dst_ref=dst, send_sem=p1_send.at[t, i * HX + xh], recv_sem=p1_recv.at[t, half],
                    device_id=(blk_at(xd), yh), device_id_type=MESH,
                )
                copy.wait_send() if wait else copy.start()

            if not wait:

                @pl.when(own)
                def _():
                    pltpu.make_async_copy(src, dst, p1_recv.at[t, half]).start()

    def q_copy(i, wait):
        yh = (y + 4 + i) & 7
        for xh in range(HX):
            own = (xh == x) & (yh == y)
            src = qin.at[:, pl.ds(pl.multiple_of((yh * HX + xh) * HD, HD), HD)]
            dst = qbuf.at[x, pl.ds(pl.multiple_of(y * PART, 32), PART)]

            @pl.when(jnp.logical_not(own))
            def _():
                copy = pltpu.make_async_remote_copy(
                    src_ref=src, dst_ref=dst, send_sem=p1_send.at[2, i * HX + xh], recv_sem=q_recv.at[0],
                    device_id=(blk_at(xh), yh), device_id_type=MESH,
                )
                copy.wait_send() if wait else copy.start()

            if not wait:

                @pl.when(own)
                def _():
                    pltpu.make_async_copy(src, dst, q_recv.at[0]).start()

    def each_y(body):
        def step(i, _):
            body(i)
            return 0

        lax.fori_loop(0, Y, step, 0)

    def all_rows(t, wait):
        @pl.when(r == 0)
        def _():
            each_y(lambda i: rows_copy(t, i, 3, wait))

        @pl.when(r != 0)
        def _():
            each_y(lambda i: rows_copy(t, i, 2, wait))

    all_rows(0, False)

    def list_copy(j):
        return pltpu.make_async_remote_copy(
            src_ref=lsend, dst_ref=lrecv.at[x], send_sem=l_send.at[j - 1], recv_sem=l_recv.at[j - 1],
            device_id=(blk_at((x + j) % X), y), device_id_type=MESH,
        )

    def list_arrival(j):
        return pltpu.make_async_remote_copy(
            src_ref=lsend, dst_ref=lrecv.at[(x + X - j) % X], send_sem=l_send.at[j - 1], recv_sem=l_recv.at[j - 1],
            device_id=(blk_at((x + j) % X), y), device_id_type=MESH,
        )

    for j in range(1, X):
        list_copy(j).start()

    def ring_copy(t, way, part, k, distance):
        n, at, size = part
        origin = (z + (Z - distance if way == 0 else distance)) & 7
        rows = region(t, origin, c, at, size)
        return pltpu.make_async_remote_copy(
            src_ref=rows, dst_ref=rows, send_sem=ring_send.at[t, way, n, k - 1], recv_sem=ring_recv.at[t, way, n, k - 1],
            device_id=(right, left)[way], device_id_type=MESH,
        )

    def sibling(t, shift, part, core):
        n, at, size = part
        rows = region(t, (z + shift) & 7, core, at, size)
        return pltpu.make_async_remote_copy(
            src_ref=rows, dst_ref=rows, send_sem=sib_send.at[t, shift, n], recv_sem=sib_recv.at[t, shift, n],
            device_id=other, device_id_type=MESH,
        )

    def guest(t, shift):
        origin = (z + shift) & 7
        return pltpu.make_async_remote_copy(
            src_ref=region(t, origin, c, GUEST, 2 * GROUPS), dst_ref=region(t, origin, c, LATE + GROUPS * x, 2 * GROUPS),
            send_sem=dl_send.at[t, shift, 0], recv_sem=dl_recv.at[t, shift, x >> 1],
            device_id=(blk_at(1), y), device_id_type=MESH,
        )

    def hand_over(t, shift, part):
        n, at, size = part
        origin = (z + shift) & 7
        return pltpu.make_async_remote_copy(
            src_ref=region(t, origin, c, at, size), dst_ref=region(t, origin, c, LATE, size),
            send_sem=dl_send.at[t, shift, n], recv_sem=dl_recv.at[t, shift, 0],
            device_id=(blk_at(2 * n), y), device_id_type=MESH,
        )

    def late_sibling(role, t, shift, core):
        rows = region(t, (z + shift) & 7, core, LATE, (18, 12)[role])
        return pltpu.make_async_remote_copy(
            src_ref=rows, dst_ref=rows, send_sem=ds_send.at[t, shift], recv_sem=ds_recv.at[t, shift],
            device_id=other, device_id_type=MESH,
        )

    def spread(role, t, shift, part):
        if role == HELP:
            hand_over(t, shift, part).start()
        elif part[0] == 2:
            guest(t, shift).start()
        else:
            sibling(t, shift, part, c).start()

    def late(role, t, shift):
        size = (18, 6)[role]
        for n in range((1, 2)[role]):
            rows = region(t, (z + shift) & 7, c, LATE + size * n, size)
            pltpu.make_async_copy(rows, rows, dl_recv.at[t, shift, n]).wait()
        late_sibling(role, t, shift, c).start()

    def late_pair(role, t, k):
        late(role, t, k)
        late(role, t, Z - k)

    def own_part(role, t):
        for part in PARTS[role]:
            n, at, size = part
            rows = region(t, z, c, at, size)
            pltpu.make_async_copy(rows, rows, p1_recv.at[t, n]).wait()
            for way in (0, 1):
                ring_copy(t, way, part, 1, 0).start()
            spread(role, t, 0, part)

    def pass_on(role, t, k, parts=(0, 1, 2)):
        for part in PARTS[role]:
            n = part[0]
            if n not in parts:
                continue
            for way in (0, 1):
                last = HOPS[n][way]
                if isinstance(k, int) and k > last:
                    continue
                ring_copy(t, way, part, k, k).wait_recv()
                if isinstance(k, int):
                    if k < last:
                        ring_copy(t, way, part, k + 1, k).start()
                elif last == 4:
                    ring_copy(t, way, part, k + 1, k).start()
                else:

                    @pl.when(k < last)
                    def _():
                        ring_copy(t, way, part, k + 1, k).start()

                spread(role, t, (Z - k) if way == 0 else k, part)

    def ring_sent(role, t):
        for part in PARTS[role]:
            for way in (0, 1):
                for k in range(1, HOPS[part[0]][way] + 1):
                    ring_copy(t, way, part, k, k - 1).wait_send()
            for shift in range(Z):
                if role == HELP:
                    hand_over(t, shift, part).wait_send()
                elif part[0] == 2:
                    guest(t, shift).wait_send()
                else:
                    sibling(t, shift, part, c).wait_send()
        if role != HELP:
            for shift in range(Z):
                late_sibling(role, t, shift, c).wait_send()

    def from_sibling(role, t):
        for shift in range(Z):
            for part in PARTS[role]:
                if part[0] < 2:
                    sibling(t, shift, part, 1 - c).wait_recv()
            late_sibling(role, t, shift, 1 - c).wait_recv()

    by_role(lambda role: own_part(role, 0))
    pack(1)
    all_rows(1, False)
    by_role(lambda role: pass_on(role, 0, 1, (0, 2)))
    reads[2].wait()
    each_y(lambda i: q_copy(i, False))
    by_role(lambda role: pass_on(role, 0, 1, (1,)))

    def k_ring(role):
        if role != HELP:
            late(role, 0, 0)
        for k in (2, 3):
            pass_on(role, 0, k)
            if role != HELP:
                late_pair(role, 0, k - 1)
        own_part(role, 1)
        pass_on(role, 0, 4)
        if role != HELP:
            late_pair(role, 0, 3)
            late(role, 0, 4)
            from_sibling(role, 0)

    by_role(k_ring)

    def o_copy(n, src, xq, u, xh, wait):
        dst = out_ref.at[:, pl.ds(pl.multiple_of((y * HX + xh) * HD, HD), HD)]
        own = (xq == x) & (u == y)

        @pl.when(jnp.logical_not(own))
        def _():
            copy = pltpu.make_async_remote_copy(
                src_ref=src, dst_ref=dst, send_sem=o_send.at[n], recv_sem=o_recv.at[0],
                device_id=(blk_at(xq), u), device_id_type=MESH,
            )
            copy.wait_send() if wait else copy.start()

        if not wait:

            @pl.when(own)
            def _():
                pltpu.make_async_copy(src, dst, o_recv.at[0]).start()

    @pl.when(x < HX)
    def _():
        place = jnp.where(x == 1, 16, 8)
        both = (EDGE, MID)

        def cluster(i):
            return (x + 1 + (i >> 1)) & 3, i & 1

        def gather(i, buf):
            xq, s = cluster(i)
            for j in range(SEL):
                at = lists[xq, place + 3 * s, j]
                gath[j * LIVE : (j + 1) * LIVE, :] = buf[pl.ds(at, GROUPS)].reshape(LIVE, HD)
            return xq, s

        def scores(i, _):
            xq, s = gather(i, kbuf)
            lane = lax.broadcasted_iota(jnp.int32, (1, KEYS), 1)
            end = jnp.zeros((1, KEYS), jnp.int32)
            for j in range(SEL):
                end = jnp.where(lane >= j * LIVE, fill_ref[lists[xq, 3 * s, j]] + j * LIVE, end)
            bias = jnp.where(lane < end, 0.0, -1e30)
            for n in range(3):
                rows = pl.ds(pl.multiple_of(s * CROWS + n * TILE, TILE), TILE)
                sc = lax.dot_general(
                    qbuf[xq, rows, :], gath[...], (((1,), (1,)), ((), ())), preferred_element_type=jnp.float32
                )
                sc = sc + bias
                peak = jnp.max(sc, axis=1, keepdims=True)
                w = jnp.exp2((sc - peak) * C2)
                totals[i, n * TILE : (n + 1) * TILE, :] = jnp.sum(w, axis=1, keepdims=True)
                probs[i, n * TILE : (n + 1) * TILE, :] = w.astype(jnp.bfloat16)
            return 0

        def block_piece(xq, u):
            return obuf.at[xq, pl.ds(pl.multiple_of(u * PART, 32), PART)]

        def mix(i, _):
            xq, s = gather(i, vbuf)
            for n in range(3):
                rows = pl.ds(pl.multiple_of(s * CROWS + n * TILE, TILE), TILE)
                o = jnp.dot(probs[i, n * TILE : (n + 1) * TILE, :], gath[...], preferred_element_type=jnp.float32)
                obuf[xq, rows, :] = (o / totals[i, n * TILE : (n + 1) * TILE, :]).astype(jnp.bfloat16)
            for w in range(4):
                o_copy(4 * i + w, block_piece(xq, 4 * s + w), xq, 4 * s + w, x, False)
            return 0

        for j in range(1, X):
            list_arrival(j).wait_recv()
        lrecv[pl.ds(x, 1)] = lsend[...][None]
        copy = pltpu.make_async_copy(lrecv, lists, l_copy.at[0])
        copy.start()
        copy.wait()
        pltpu.make_async_copy(qbuf, qbuf, q_recv.at[0]).wait()

        by_role(lambda role: late(role, 1, 0), both)

        def v_step(k, _):
            by_role(lambda role: pass_on(role, 1, k, (0, 2)), both)
            scores(2 * k - 2, 0)
            by_role(lambda role: pass_on(role, 1, k, (1,)), both)
            scores(2 * k - 1, 0)

            @pl.when(k > 1)
            def _():
                by_role(lambda role: late_pair(role, 1, k - 1), both)

            return 0

        lax.fori_loop(1, 4, v_step, 0)
        lax.fori_loop(6, 8, scores, 0)

        def v_end(role):
            late_pair(role, 1, 3)
            pass_on(role, 1, 4)
            late(role, 1, 4)
            from_sibling(role, 1)

        by_role(v_end, both)
        lax.fori_loop(0, 8, mix, 0)

        def done(role):
            for t in (0, 1):
                ring_sent(role, t)

        by_role(done, both)

        def sent(i, _):
            xq, s = cluster(i)
            for w in range(4):
                o_copy(4 * i + w, block_piece(xq, 4 * s + w), xq, 4 * s + w, x, True)
            return 0

        lax.fori_loop(0, 8, sent, 0)

    @pl.when(x == HX)
    def _():
        for k in range(1, 5):
            pass_on(HELP, 1, k)
        for j in range(1, X):
            list_arrival(j).wait_recv()
        for t in (0, 1):
            ring_sent(HELP, t)

    all_rows(0, True)
    all_rows(1, True)
    each_y(lambda i: q_copy(i, True))
    for j in range(1, X):
        list_copy(j).wait_send()
    pltpu.make_async_copy(out_ref, out_ref, o_recv.at[0]).wait()


def local(queries, keys, values, key_lists, key_fill):
    bf = jnp.bfloat16
    anywhere = pl.BlockSpec(memory_space=pl.ANY)
    dma = pltpu.SemaphoreType.DMA
    return pl.pallas_call(
        kernel,
        out_shape=jax.ShapeDtypeStruct(queries.shape, bf),
        in_specs=[
            anywhere, anywhere, anywhere,
            pl.BlockSpec(memory_space=pltpu.VMEM), pl.BlockSpec(memory_space=pltpu.SMEM),
        ],
        out_specs=anywhere,
        scratch_shapes=[
            pltpu.VMEM((PART, HEADS * HD), bf),
            pltpu.VMEM((PART, HEADS * HD), bf),
            pltpu.VMEM((PART, HEADS * HD), bf),
            pltpu.VMEM((HEADS, GROUPS, 32, HD), bf),
            pltpu.VMEM((HEADS, GROUPS, 32, HD), bf),
            pltpu.VMEM((Z * C * CHUNK, 32, HD), bf),
            pltpu.VMEM((Z * C * CHUNK, 32, HD), bf),
            pltpu.VMEM((X, BLOCK, HD), bf),
            pltpu.VMEM((X, BLOCK, HD), bf),
            pltpu.VMEM((KEYS, HD), bf),
            pltpu.VMEM((2 * X, CROWS, KEYS), bf),
            pltpu.VMEM((2 * X, CROWS, 1), jnp.float32),
            pltpu.VMEM((24, 128), jnp.int32),
            pltpu.VMEM((X, 24, 128), jnp.int32),
            pltpu.SMEM((X, 24, 128), jnp.int32),
            dma((3,)),
            dma((3, HEADS)),
            dma((2, 3)),
            dma((1,)),
            dma((2, 2, 3, 4)),
            dma((2, 2, 3, 4)),
            dma((2, Z, 2)),
            dma((2, Z, 2)),
            dma((2, Z, 2)),
            dma((2, Z, 2)),
            dma((2, Z)),
            dma((2, Z)),
            dma((X - 1,)),
            dma((X - 1,)),
            dma((1,)),
            dma((X * Y,)),
            dma((1,)),
        ],
        compiler_params=pltpu.CompilerParams(
            collective_id=0, has_side_effects=True, vmem_limit_bytes=56 * 1024 * 1024
        ),
        cost_estimate=pl.CostEstimate(flops=5_000_000_000, bytes_accessed=4_000_000, transcendentals=4_800_000),
    )(queries, keys, values, key_lists, key_fill)


def solution(mesh):
    in_specs = (
        P(("blk", "uly"), None),
        P(("blk", "uly"), None),
        P(("blk", "uly"), None),
        P("blk", None),
        P(),
    )
    out_specs = P(("blk", "uly"), None)
    return jax.shard_map(local, mesh=mesh, in_specs=in_specs, out_specs=out_specs, check_vma=False)
```

time: 138 us -> 131 us (0.949)
  the two profiles are of different devices: /device:TPU:55 before, /device:TPU:1 now
where the time goes in v4:
time: 131 us; the launch traced here: 130 us
  Pallas kernels  128 us (98%)
  local copies, waits for them, and re-layouts  1.92 us (1%)
    pallas_call x1, Pallas kernels, local(): pl.pallas_call(kernel, out_shape=jax.ShapeDtypeStruct(queries.shape, bf),...  128 us

profile of v4, /device:TPU:1, one launch (start us, length us, event | category | flops | bytes accessed | tf_op | source)
XLA Modules:
  0.0 130.1 jit_solution(13206867100273234894)
XLA Ops:
  0.0 128.2 %shard_map.55 = bf16[96,3072]{1,0:T(8,128)(2,1)} custom-call(bf16[96,3072]{1,0:T(8,128)(2,1)} %q_ref.1, bf16[96,3072]{1,0:T(8,128)(2,1)} %k_ref.1, bf16[96,3072]{1,0:T(8,128)(2,1)} %v_ref.1, s32[6,16]{1,0:T(8,128)} %list_ref.1, s32[384]{0:T(512)} %fill_ref.1), custom_call_target="tpu_custom_call" | custom-call | flops 5000000000 | bytes 4000000 | tf_op jit(solution)/shard_map/pallas_call | solution.py:471
  128.2 1.9 %copy.7 = bf16[96,3072]{1,0:T(8,128)(2,1)} copy(bf16[96,3072]{1,0:T(8,128)(2,1)} %shard_map.55) | data formatting | bytes 1179648

commit v5 on v4

--- a/solution.py
+++ b/solution.py
@@ -33,7 +33,7 @@
 
 def kernel(
     q_ref, k_ref, v_ref, list_ref, fill_ref, out_ref,
-    qin, kin, vin, kpack, vpack, kbuf, vbuf, qbuf, obuf, gath, probs, totals, lsend, lrecv, lists,
+    qin, kin, vin, kpack, vpack0, vpack1, kbuf, vbuf0, vbuf1, qbuf, obuf, oin, gath, probs, totals, lsend, lrecv, lists,
     in_sem, p1_send, p1_recv, q_recv, ring_send, ring_recv, sib_send, sib_recv, dl_send, dl_recv, ds_send, ds_recv,
     l_send, l_recv, l_copy, o_send, o_recv,
 ):
@@ -83,19 +83,34 @@
     piece0 = pl.multiple_of(jnp.where(r == 1, 32, 0), 32)
     piece1 = pl.multiple_of(jnp.where((r == 1) | (r == 2), 64, 32), 32)
 
-    def pack(t):
-        src, dst = ((kin, kpack), (vin, vpack))[t]
-        reads[t].wait()
+    def pieces(src, h):
+        cols = slice(h * HD, (h + 1) * HD)
+        return src[pl.ds(piece0, 32), cols], src[pl.ds(piece1, 32), cols], src[64:96, cols]
+
+    def pack_k():
+        reads[0].wait()
         for h in range(HEADS):
-            cols = slice(h * HD, (h + 1) * HD)
-            dst[h, 0] = src[pl.ds(piece0, 32), cols]
-            dst[h, 1] = src[pl.ds(piece1, 32), cols]
-            dst[h, 2] = src[64:96, cols]
-
-    pack(0)
+            for g, rows in enumerate(pieces(kin, h)):
+                kpack[h, g] = rows
+
+    def paired(top, bottom):
+        left = lax.broadcasted_iota(jnp.int32, top.shape, 1) < HD // 2
+        return (
+            jnp.where(left, top, pltpu.roll(bottom, HD // 2, 1)).astype(jnp.bfloat16),
+            jnp.where(left, pltpu.roll(top, HD // 2, 1), bottom).astype(jnp.bfloat16),
+        )
+
+    def pack_v():
+        reads[1].wait()
+        for h in range(HEADS):
+            for g, rows in enumerate(pieces(vin, h)):
+                rows = rows.astype(jnp.float32)
+                vpack0[h, g], vpack1[h, g] = paired(rows[0:16], rows[16:32])
+
+    pack_k()
     pl.semaphore_wait(barrier, len(near) + 3)
 
-    bufs = (kbuf, vbuf)
+    bufs = (kbuf, vbuf0, vbuf1)
 
     def region(t, zz, core, at, count):
         return bufs[t].at[pl.ds((zz * C + core) * CHUNK + at, count)]
@@ -124,7 +139,7 @@
         yh = (y + 4 + i) & 7
         for xh, (xd, at, half) in enumerate(targets):
             own = (xd == x) & (yh == y)
-            src = (kpack, vpack)[t].at[yh * HX + xh, pl.ds(0, rows)]
+            src = (kpack, vpack0, vpack1)[t].at[yh * HX + xh, pl.ds(0, rows)]
             dst = region(t, z, c, at, rows)
 
             @pl.when(jnp.logical_not(own))
@@ -151,7 +166,7 @@
             @pl.when(jnp.logical_not(own))
             def _():
                 copy = pltpu.make_async_remote_copy(
-                    src_ref=src, dst_ref=dst, send_sem=p1_send.at[2, i * HX + xh], recv_sem=q_recv.at[0],
+                    src_ref=src, dst_ref=dst, send_sem=p1_send.at[3, i * HX + xh], recv_sem=q_recv.at[0],
                     device_id=(blk_at(xh), yh), device_id_type=MESH,
                 )
                 copy.wait_send() if wait else copy.start()
@@ -200,7 +215,7 @@
         origin = (z + (Z - distance if way == 0 else distance)) & 7
         rows = region(t, origin, c, at, size)
         return pltpu.make_async_remote_copy(
-            src_ref=rows, dst_ref=rows, send_sem=ring_send.at[t, way, n, k - 1], recv_sem=ring_recv.at[t, way, n, k - 1],
+            src_ref=rows, dst_ref=rows, send_sem=ring_send.at[t], recv_sem=ring_recv.at[t, way, n, k - 1],
             device_id=(right, left)[way], device_id_type=MESH,
         )
 
@@ -208,7 +223,7 @@
         n, at, size = part
         rows = region(t, (z + shift) & 7, core, at, size)
         return pltpu.make_async_remote_copy(
-            src_ref=rows, dst_ref=rows, send_sem=sib_send.at[t, shift, n], recv_sem=sib_recv.at[t, shift, n],
+            src_ref=rows, dst_ref=rows, send_sem=sib_send.at[t], recv_sem=sib_recv.at[t, shift, n],
             device_id=other, device_id_type=MESH,
         )
 
@@ -216,7 +231,7 @@
         origin = (z + shift) & 7
         return pltpu.make_async_remote_copy(
             src_ref=region(t, origin, c, GUEST, 2 * GROUPS), dst_ref=region(t, origin, c, LATE + GROUPS * x, 2 * GROUPS),
-            send_sem=dl_send.at[t, shift, 0], recv_sem=dl_recv.at[t, shift, x >> 1],
+            send_sem=dl_send.at[t], recv_sem=dl_recv.at[t, shift, x >> 1],
             device_id=(blk_at(1), y), device_id_type=MESH,
         )
 
@@ -225,14 +240,14 @@
         origin = (z + shift) & 7
         return pltpu.make_async_remote_copy(
             src_ref=region(t, origin, c, at, size), dst_ref=region(t, origin, c, LATE, size),
-            send_sem=dl_send.at[t, shift, n], recv_sem=dl_recv.at[t, shift, 0],
+            send_sem=dl_send.at[t], recv_sem=dl_recv.at[t, shift, 0],
             device_id=(blk_at(2 * n), y), device_id_type=MESH,
         )
 
     def late_sibling(role, t, shift, core):
         rows = region(t, (z + shift) & 7, core, LATE, (18, 12)[role])
         return pltpu.make_async_remote_copy(
-            src_ref=rows, dst_ref=rows, send_sem=ds_send.at[t, shift], recv_sem=ds_recv.at[t, shift],
+            src_ref=rows, dst_ref=rows, send_sem=ds_send.at[t], recv_sem=ds_recv.at[t, shift],
             device_id=other, device_id_type=MESH,
         )
 
@@ -287,21 +302,21 @@
 
                 spread(role, t, (Z - k) if way == 0 else k, part)
 
+    def sent_all(t, sem, groups):
+        rows = bufs[t].at[pl.ds(0, groups)]
+        pltpu.make_async_copy(rows, rows, sem.at[t]).wait()
+
     def ring_sent(role, t):
-        for part in PARTS[role]:
-            for way in (0, 1):
-                for k in range(1, HOPS[part[0]][way] + 1):
-                    ring_copy(t, way, part, k, k - 1).wait_send()
-            for shift in range(Z):
-                if role == HELP:
-                    hand_over(t, shift, part).wait_send()
-                elif part[0] == 2:
-                    guest(t, shift).wait_send()
-                else:
-                    sibling(t, shift, part, c).wait_send()
-        if role != HELP:
-            for shift in range(Z):
-                late_sibling(role, t, shift, c).wait_send()
+        sizes = [size for n, _, size in PARTS[role] if n < 2]
+        guests = 6 if role == EDGE else 0
+        sent_all(t, ring_send, (sum(sizes) + guests) * (Z - 1))
+        if role == HELP:
+            sent_all(t, dl_send, sum(sizes) * Z)
+            return
+        sent_all(t, sib_send, sum(sizes) * Z)
+        sent_all(t, ds_send, (18, 12)[role] * Z)
+        if guests:
+            sent_all(t, dl_send, guests * Z)
 
     def from_sibling(role, t):
         for shift in range(Z):
@@ -310,38 +325,46 @@
                     sibling(t, shift, part, 1 - c).wait_recv()
             late_sibling(role, t, shift, 1 - c).wait_recv()
 
+    pack_v()
     by_role(lambda role: own_part(role, 0))
-    pack(1)
     all_rows(1, False)
     by_role(lambda role: pass_on(role, 0, 1, (0, 2)))
     reads[2].wait()
     each_y(lambda i: q_copy(i, False))
     by_role(lambda role: pass_on(role, 0, 1, (1,)))
 
+    def turn(role, t):
+        pass_on(role, t + 1, 1)
+        pass_on(role, t, 4)
+        if role != HELP:
+            late_pair(role, t, 3)
+            late(role, t, 4)
+            from_sibling(role, t)
+            late(role, t + 1, 0)
+
+    by_role(lambda role: pass_on(role, 0, 2))
+    all_rows(2, False)
+
     def k_ring(role):
+        own_part(role, 1)
         if role != HELP:
             late(role, 0, 0)
-        for k in (2, 3):
-            pass_on(role, 0, k)
-            if role != HELP:
-                late_pair(role, 0, k - 1)
-        own_part(role, 1)
-        pass_on(role, 0, 4)
+            late_pair(role, 0, 1)
+        pass_on(role, 0, 3)
         if role != HELP:
-            late_pair(role, 0, 3)
-            late(role, 0, 4)
-            from_sibling(role, 0)
+            late_pair(role, 0, 2)
+        turn(role, 0)
 
     by_role(k_ring)
 
-    def o_copy(n, src, xq, u, xh, wait):
-        dst = out_ref.at[:, pl.ds(pl.multiple_of((y * HX + xh) * HD, HD), HD)]
+    def o_copy(half, n, xq, u, wait):
+        src, dst = obuf.at[half, xq, u], oin.at[half, y * HX + x]
         own = (xq == x) & (u == y)
 
         @pl.when(jnp.logical_not(own))
         def _():
             copy = pltpu.make_async_remote_copy(
-                src_ref=src, dst_ref=dst, send_sem=o_send.at[n], recv_sem=o_recv.at[0],
+                src_ref=src, dst_ref=dst, send_sem=o_send.at[half, n], recv_sem=o_recv.at[half],
                 device_id=(blk_at(xq), u), device_id_type=MESH,
             )
             copy.wait_send() if wait else copy.start()
@@ -350,7 +373,7 @@
 
             @pl.when(own)
             def _():
-                pltpu.make_async_copy(src, dst, o_recv.at[0]).start()
+                pltpu.make_async_copy(src, dst, o_recv.at[half]).start()
 
     @pl.when(x < HX)
     def _():
@@ -364,16 +387,22 @@
             xq, s = cluster(i)
             for j in range(SEL):
                 at = lists[xq, place + 3 * s, j]
-                gath[j * LIVE : (j + 1) * LIVE, :] = buf[pl.ds(at, GROUPS)].reshape(LIVE, HD)
+                for n in range(buf.shape[1] // 16):
+                    row = n * (KEYS // 2) + j * (LIVE // 2)
+                    gath[row : row + LIVE // 2, :] = buf[pl.ds(at, GROUPS), n * 16 : (n + 1) * 16, :].reshape(LIVE // 2, HD)
             return xq, s
 
         def scores(i, _):
             xq, s = gather(i, kbuf)
             lane = lax.broadcasted_iota(jnp.int32, (1, KEYS), 1)
+            low = jnp.where(lane >= KEYS // 2, 1, 0)
+            at = lane - low * (KEYS // 2)
+            n = at - ((at * 1366) >> 16) * (LIVE // 2)
+            row = ((n >> 4) << 5) + (n & 15) + 16 * low
             end = jnp.zeros((1, KEYS), jnp.int32)
             for j in range(SEL):
-                end = jnp.where(lane >= j * LIVE, fill_ref[lists[xq, 3 * s, j]] + j * LIVE, end)
-            bias = jnp.where(lane < end, 0.0, -1e30)
+                end = jnp.where(at >= j * (LIVE // 2), fill_ref[lists[xq, 3 * s, j]], end)
+            bias = jnp.where(row < end, 0.0, -1e30)
             for n in range(3):
                 rows = pl.ds(pl.multiple_of(s * CROWS + n * TILE, TILE), TILE)
                 sc = lax.dot_general(
@@ -386,18 +415,38 @@
                 probs[i, n * TILE : (n + 1) * TILE, :] = w.astype(jnp.bfloat16)
             return 0
 
-        def block_piece(xq, u):
-            return obuf.at[xq, pl.ds(pl.multiple_of(u * PART, 32), PART)]
-
-        def mix(i, _):
-            xq, s = gather(i, vbuf)
-            for n in range(3):
-                rows = pl.ds(pl.multiple_of(s * CROWS + n * TILE, TILE), TILE)
-                o = jnp.dot(probs[i, n * TILE : (n + 1) * TILE, :], gath[...], preferred_element_type=jnp.float32)
-                obuf[xq, rows, :] = (o / totals[i, n * TILE : (n + 1) * TILE, :]).astype(jnp.bfloat16)
+        def mix(half, i):
+            xq, s = gather(i, (vbuf0, vbuf1)[half])
             for w in range(4):
-                o_copy(4 * i + w, block_piece(xq, 4 * s + w), xq, 4 * s + w, x, False)
+                rows = slice(w * PART, (w + 1) * PART)
+                top = jnp.dot(probs[i, rows, : KEYS // 2], gath[: KEYS // 2, :], preferred_element_type=jnp.float32)
+                low = jnp.dot(probs[i, rows, KEYS // 2 :], gath[: KEYS // 2, :], preferred_element_type=jnp.float32)
+                if half:
+                    o = pltpu.roll(top, HD // 2, 1) + low
+                else:
+                    o = top + pltpu.roll(low, HD // 2, 1)
+                o = o / totals[i, rows, :]
+                obuf[half, xq, 4 * s + w] = paired(o[: PART // 2], o[PART // 2 :])[half]
+            for w in range(4):
+                o_copy(half, 4 * i + w, xq, 4 * s + w, False)
             return 0
+
+        def v_step(t, work):
+            def step(k, _):
+                by_role(lambda role: pass_on(role, t, k, (0, 2)), both)
+                lax.fori_loop(4 * k - 8, 4 * k - 6, work, 0)
+                by_role(lambda role: pass_on(role, t, k, (1,)), both)
+                if t == 1:
+
+                    @pl.when(k == 2)
+                    def _():
+                        by_role(lambda role: own_part(role, 2), both)
+
+                lax.fori_loop(4 * k - 6, 4 * k - 4, work, 0)
+                by_role(lambda role: late_pair(role, t, k - 1), both)
+                return 0
+
+            return step
 
         for j in range(1, X):
             list_arrival(j).wait_recv()
@@ -407,61 +456,59 @@
         copy.wait()
         pltpu.make_async_copy(qbuf, qbuf, q_recv.at[0]).wait()
 
-        by_role(lambda role: late(role, 1, 0), both)
-
-        def v_step(k, _):
-            by_role(lambda role: pass_on(role, 1, k, (0, 2)), both)
-            scores(2 * k - 2, 0)
-            by_role(lambda role: pass_on(role, 1, k, (1,)), both)
-            scores(2 * k - 1, 0)
-
-            @pl.when(k > 1)
-            def _():
-                by_role(lambda role: late_pair(role, 1, k - 1), both)
-
-            return 0
-
-        lax.fori_loop(1, 4, v_step, 0)
-        lax.fori_loop(6, 8, scores, 0)
+        lax.fori_loop(2, 4, v_step(1, scores), 0)
+        by_role(lambda role: turn(role, 1), both)
+        lax.fori_loop(2, 4, v_step(2, lambda i, _: mix(0, i)), 0)
 
         def v_end(role):
-            late_pair(role, 1, 3)
-            pass_on(role, 1, 4)
-            late(role, 1, 4)
-            from_sibling(role, 1)
+            late_pair(role, 2, 3)
+            pass_on(role, 2, 4)
+            late(role, 2, 4)
+            from_sibling(role, 2)
 
         by_role(v_end, both)
-        lax.fori_loop(0, 8, mix, 0)
+        lax.fori_loop(0, 8, lambda i, _: mix(1, i), 0)
 
         def done(role):
-            for t in (0, 1):
+            for t in (0, 1, 2):
                 ring_sent(role, t)
 
         by_role(done, both)
 
         def sent(i, _):
             xq, s = cluster(i)
-            for w in range(4):
-                o_copy(4 * i + w, block_piece(xq, 4 * s + w), xq, 4 * s + w, x, True)
+            for half in (0, 1):
+                for w in range(4):
+                    o_copy(half, 4 * i + w, xq, 4 * s + w, True)
             return 0
 
         lax.fori_loop(0, 8, sent, 0)
 
     @pl.when(x == HX)
     def _():
-        for k in range(1, 5):
-            pass_on(HELP, 1, k)
+        pass_on(HELP, 1, 2)
+        own_part(HELP, 2)
+        pass_on(HELP, 1, 3)
+        turn(HELP, 1)
+        for k in range(2, 5):
+            pass_on(HELP, 2, k)
         for j in range(1, X):
             list_arrival(j).wait_recv()
-        for t in (0, 1):
+        for t in (0, 1, 2):
             ring_sent(HELP, t)
 
-    all_rows(0, True)
-    all_rows(1, True)
+    for t in (0, 1, 2):
+        all_rows(t, True)
     each_y(lambda i: q_copy(i, True))
     for j in range(1, X):
         list_copy(j).wait_send()
-    pltpu.make_async_copy(out_ref, out_ref, o_recv.at[0]).wait()
+    for half in (0, 1):
+        pltpu.make_async_copy(oin.at[half], oin.at[half], o_recv.at[half]).wait()
+    for h in range(HEADS):
+        cols = slice(h * HD, (h + 1) * HD)
+        out_ref[0 : PART // 2, cols], out_ref[PART // 2 :, cols] = paired(
+            oin[0, h].astype(jnp.float32), oin[1, h].astype(jnp.float32)
+        )
 
 
 def local(queries, keys, values, key_lists, key_fill):
@@ -475,17 +522,20 @@
             anywhere, anywhere, anywhere,
             pl.BlockSpec(memory_space=pltpu.VMEM), pl.BlockSpec(memory_space=pltpu.SMEM),
         ],
-        out_specs=anywhere,
+        out_specs=pl.BlockSpec(memory_space=pltpu.VMEM),
         scratch_shapes=[
             pltpu.VMEM((PART, HEADS * HD), bf),
             pltpu.VMEM((PART, HEADS * HD), bf),
             pltpu.VMEM((PART, HEADS * HD), bf),
             pltpu.VMEM((HEADS, GROUPS, 32, HD), bf),
-            pltpu.VMEM((HEADS, GROUPS, 32, HD), bf),
+            pltpu.VMEM((HEADS, GROUPS, 16, HD), bf),
+            pltpu.VMEM((HEADS, GROUPS, 16, HD), bf),
             pltpu.VMEM((Z * C * CHUNK, 32, HD), bf),
-            pltpu.VMEM((Z * C * CHUNK, 32, HD), bf),
+            pltpu.VMEM((Z * C * CHUNK, 16, HD), bf),
+            pltpu.VMEM((Z * C * CHUNK, 16, HD), bf),
             pltpu.VMEM((X, BLOCK, HD), bf),
-            pltpu.VMEM((X, BLOCK, HD), bf),
+            pltpu.VMEM((2, X, Y, PART // 2, HD), bf),
+            pltpu.VMEM((2, HEADS, PART // 2, HD), bf),
             pltpu.VMEM((KEYS, HD), bf),
             pltpu.VMEM((2 * X, CROWS, KEYS), bf),
             pltpu.VMEM((2 * X, CROWS, 1), jnp.float32),
@@ -493,22 +543,22 @@
             pltpu.VMEM((X, 24, 128), jnp.int32),
             pltpu.SMEM((X, 24, 128), jnp.int32),
             dma((3,)),
-            dma((3, HEADS)),
-            dma((2, 3)),
+            dma((4, HEADS)),
+            dma((3, 3)),
             dma((1,)),
-            dma((2, 2, 3, 4)),
-            dma((2, 2, 3, 4)),
-            dma((2, Z, 2)),
-            dma((2, Z, 2)),
-            dma((2, Z, 2)),
-            dma((2, Z, 2)),
-            dma((2, Z)),
-            dma((2, Z)),
+            dma((3,)),
+            dma((3, 2, 3, 4)),
+            dma((3,)),
+            dma((3, Z, 2)),
+            dma((3,)),
+            dma((3, Z, 2)),
+            dma((3,)),
+            dma((3, Z)),
             dma((X - 1,)),
             dma((X - 1,)),
             dma((1,)),
-            dma((X * Y,)),
-            dma((1,)),
+            dma((2, X * Y)),
+            dma((2,)),
         ],
         compiler_params=pltpu.CompilerParams(
             collective_id=0, has_side_effects=True, vmem_limit_bytes=56 * 1024 * 1024

time: 131 us -> 127 us (0.969)
  Pallas kernels: 128 us -> 124 us
    pallas_call x1, Pallas kernels: 128 us -> 124 us  [local(): pl.pallas_call(kernel, out_shape=jax.ShapeDtypeStruct(queries.shape, bf),...]
where the time goes in v5:
time: 127 us; the launch traced here: 126 us
  Pallas kernels  124 us (98%)
  local copies, waits for them, and re-layouts  1.92 us (2%)
    pallas_call x1, Pallas kernels, local(): pl.pallas_call(kernel, out_shape=jax.ShapeDtypeStruct(queries.shape, bf),...  124 us

profile of v5, /device:TPU:1, one launch (start us, length us, event | category | flops | bytes accessed | tf_op | source)
XLA Modules:
  0.0 126.4 jit_solution(3870221161579420672)
XLA Ops:
  0.0 124.5 %shard_map.55 = bf16[96,3072]{1,0:T(8,128)(2,1)} custom-call(bf16[96,3072]{1,0:T(8,128)(2,1)} %q_ref.1, bf16[96,3072]{1,0:T(8,128)(2,1)} %k_ref.1, bf16[96,3072]{1,0:T(8,128)(2,1)} %v_ref.1, s32[6,16]{1,0:T(8,128)} %list_ref.1, s32[384]{0:T(512)} %fill_ref.1), custom_call_target="tpu_custom_call" | custom-call | flops 5000000000 | bytes 4000000 | tf_op jit(solution)/shard_map/pallas_call | solution.py:518
  124.5 1.9 %copy.7 = bf16[96,3072]{1,0:T(8,128)(2,1)} copy(bf16[96,3072]{1,0:T(8,128)(2,1)} %shard_map.55) | data formatting | bytes 1179648

commit v6 on v5

--- a/solution.py
+++ b/solution.py
@@ -32,7 +32,7 @@
 
 
 def kernel(
-    q_ref, k_ref, v_ref, list_ref, fill_ref, out_ref,
+    q_ref, k_ref, v_ref, list_hbm, fill_hbm, out_ref, list_ref, fill_ref,
     qin, kin, vin, kpack, vpack0, vpack1, kbuf, vbuf0, vbuf1, qbuf, obuf, oin, gath, probs, totals, lsend, lrecv, lists,
     in_sem, p1_send, p1_recv, q_recv, ring_send, ring_recv, sib_send, sib_recv, dl_send, dl_recv, ds_send, ds_recv,
     l_send, l_recv, l_copy, o_send, o_recv,
@@ -49,7 +49,7 @@
 
     reads = [
         pltpu.make_async_copy(src, dst, in_sem.at[n])
-        for n, (src, dst) in enumerate(((k_ref, kin), (v_ref, vin), (q_ref, qin)))
+        for n, (src, dst) in enumerate(((k_ref, kin), (v_ref, vin), (q_ref, qin), (list_hbm, list_ref), (fill_hbm, fill_ref)))
     ]
     for copy in reads:
         copy.start()
@@ -61,10 +61,132 @@
     right = ((blk & 49) + (((z + 1) & 7) << 1), y)
     left = ((blk & 49) + (((z + 7) & 7) << 1), y)
     other = (blk ^ 1, y)
-    near = [(blk_at((x + i) & 3), (y + j) & 7) for j in range(Y) for i in range(X) if i or j]
-    for d in (right, left, other, *near):
+    steps = [(i, j) for j in range(Y) for i in range(X) if i or j]
+    steps.sort(key=lambda ij: -min(ij[0], X - ij[0]) - min(ij[1], Y - ij[1]))
+    near = [(blk_at((x + i) & 3), (y + j) & 7) for i, j in steps]
+    for d in (*near, right, left, other):
         pl.semaphore_signal(barrier, inc=1, device_id=d, device_id_type=MESH)
 
+    piece0 = pl.multiple_of(jnp.where(r == 1, 32, 0), 32)
+    piece1 = pl.multiple_of(jnp.where((r == 1) | (r == 2), 64, 32), 32)
+
+    def pieces(src, h):
+        cols = slice(h * HD, (h + 1) * HD)
+        return src[pl.ds(piece0, 32), cols], src[pl.ds(piece1, 32), cols], src[64:96, cols]
+
+    def pack_k():
+        reads[0].wait()
+        for h in range(HEADS):
+            for g, rows in enumerate(pieces(kin, h)):
+                kpack[h, g] = rows
+
+    def paired(top, bottom):
+        left = lax.broadcasted_iota(jnp.int32, top.shape, 1) < HD // 2
+        return (
+            jnp.where(left, top, pltpu.roll(bottom, HD // 2, 1)).astype(jnp.bfloat16),
+            jnp.where(left, pltpu.roll(top, HD // 2, 1), bottom).astype(jnp.bfloat16),
+        )
+
+    def pack_v():
+        reads[1].wait()
+        for h in range(HEADS):
+            for g, rows in enumerate(pieces(vin, h)):
+                rows = rows.astype(jnp.float32)
+                vpack0[h, g], vpack1[h, g] = paired(rows[0:16], rows[16:32])
+
+    pack_k()
+    pl.semaphore_wait(barrier, len(near) + 3)
+
+    bufs = (kbuf, vbuf0, vbuf1)
+
+    def region(t, zz, core, at, count):
+        return bufs[t].at[pl.ds((zz * C + core) * CHUNK + at, count)]
+
+    off = jnp.where(r == 0, 0, 1 + 2 * r)
+    wing = (x == 0) | (x == 2)
+    i32 = jnp.int32
+
+    def target(xh):
+        if xh != 1:
+            helped = x == 3
+            xd = jnp.where(helped, 3, xh)
+            at = jnp.where(helped, (PER if xh else 0), x * PER) * GROUPS + 9 * a + off
+            half = jnp.where(helped, xh // 2, jnp.where((x == 2) | ((x == 1) & (a == 1) & (r != 0)), 1, 0))
+            return xd, at, half
+        guest = wing & (r == 0)
+        xd = jnp.where(guest, x, 1)
+        own = jnp.where(wing, 5 * x * GROUPS + 6 * a + off - 3, jnp.where(x == 1, 4, 14) * GROUPS + 9 * a + off)
+        at = jnp.where(guest, GUEST + GROUPS * a, own)
+        half = jnp.where(guest, 2, jnp.where(x >= 2, 1, 0))
+        return xd, at, half
+
+    targets = [target(xh) for xh in range(HX)]
+
+    def far_first(i):
+        return (y + jnp.where(i & 1 == 1, 4 - ((i + 1) >> 1), 4 + (i >> 1))) & 7
+
+    def rows_copy(t, i, rows, wait):
+        yh = far_first(i)
+        for xh, (xd, at, half) in enumerate(targets):
+            own = (xd == x) & (yh == y)
+            src = (kpack, vpack0, vpack1)[t].at[yh * HX + xh, pl.ds(0, rows)]
+            dst = region(t, z, c, at, rows)
+
+            @pl.when(jnp.logical_not(own))
+            def _():
+                copy = pltpu.make_async_remote_copy(
+                    src_ref=src, dst_ref=dst, send_sem=p1_send.at[t, i * HX + xh], recv_sem=p1_recv.at[t, half],
+                    device_id=(blk_at(xd), yh), device_id_type=MESH,
+                )
+                copy.wait_send() if wait else copy.start()
+
+            if not wait:
+
+                @pl.when(own)
+                def _():
+                    pltpu.make_async_copy(src, dst, p1_recv.at[t, half]).start()
+
+    def q_copy(i, wait):
+        yh = far_first(i)
+        for xh in range(HX):
+            own = (xh == x) & (yh == y)
+            src = qin.at[:, pl.ds(pl.multiple_of((yh * HX + xh) * HD, HD), HD)]
+            dst = qbuf.at[x, pl.ds(pl.multiple_of(y * PART, 32), PART)]
+
+            @pl.when(jnp.logical_not(own))
+            def _():
+                copy = pltpu.make_async_remote_copy(
+                    src_ref=src, dst_ref=dst, send_sem=p1_send.at[3, i * HX + xh], recv_sem=q_recv.at[0],
+                    device_id=(blk_at(xh), yh), device_id_type=MESH,
+                )
+                copy.wait_send() if wait else copy.start()
+
+            if not wait:
+
+                @pl.when(own)
+                def _():
+                    pltpu.make_async_copy(src, dst, q_recv.at[0]).start()
+
+    def each_y(body):
+        def step(i, _):
+            body(i)
+            return 0
+
+        lax.fori_loop(0, Y, step, 0)
+
+    def all_rows(t, wait):
+        @pl.when(r == 0)
+        def _():
+            each_y(lambda i: rows_copy(t, i, 3, wait))
+
+        @pl.when(r != 0)
+        def _():
+            each_y(lambda i: rows_copy(t, i, 2, wait))
+
+    all_rows(0, False)
+
+    reads[3].wait()
+    reads[4].wait()
     lsend[...] = jnp.zeros_like(lsend)
     tile = list_ref[...]
     owner = (tile * 10923) >> 16
@@ -79,121 +201,6 @@
     lsend[0:PER, 0:SEL] = tile
     lsend[8 : 8 + PER, 0:SEL] = (start + edge) * GROUPS
     lsend[16 : 16 + PER, 0:SEL] = (start + middle) * GROUPS
-
-    piece0 = pl.multiple_of(jnp.where(r == 1, 32, 0), 32)
-    piece1 = pl.multiple_of(jnp.where((r == 1) | (r == 2), 64, 32), 32)
-
-    def pieces(src, h):
-        cols = slice(h * HD, (h + 1) * HD)
-        return src[pl.ds(piece0, 32), cols], src[pl.ds(piece1, 32), cols], src[64:96, cols]
-
-    def pack_k():
-        reads[0].wait()
-        for h in range(HEADS):
-            for g, rows in enumerate(pieces(kin, h)):
-                kpack[h, g] = rows
-
-    def paired(top, bottom):
-        left = lax.broadcasted_iota(jnp.int32, top.shape, 1) < HD // 2
-        return (
-            jnp.where(left, top, pltpu.roll(bottom, HD // 2, 1)).astype(jnp.bfloat16),
-            jnp.where(left, pltpu.roll(top, HD // 2, 1), bottom).astype(jnp.bfloat16),
-        )
-
-    def pack_v():
-        reads[1].wait()
-        for h in range(HEADS):
-            for g, rows in enumerate(pieces(vin, h)):
-                rows = rows.astype(jnp.float32)
-                vpack0[h, g], vpack1[h, g] = paired(rows[0:16], rows[16:32])
-
-    pack_k()
-    pl.semaphore_wait(barrier, len(near) + 3)
-
-    bufs = (kbuf, vbuf0, vbuf1)
-
-    def region(t, zz, core, at, count):
-        return bufs[t].at[pl.ds((zz * C + core) * CHUNK + at, count)]
-
-    off = jnp.where(r == 0, 0, 1 + 2 * r)
-    wing = (x == 0) | (x == 2)
-    i32 = jnp.int32
-
-    def target(xh):
-        if xh != 1:
-            helped = x == 3
-            xd = jnp.where(helped, 3, xh)
-            at = jnp.where(helped, (PER if xh else 0), x * PER) * GROUPS + 9 * a + off
-            half = jnp.where(helped, xh // 2, jnp.where((x == 2) | ((x == 1) & (a == 1) & (r != 0)), 1, 0))
-            return xd, at, half
-        guest = wing & (r == 0)
-        xd = jnp.where(guest, x, 1)
-        own = jnp.where(wing, 5 * x * GROUPS + 6 * a + off - 3, jnp.where(x == 1, 4, 14) * GROUPS + 9 * a + off)
-        at = jnp.where(guest, GUEST + GROUPS * a, own)
-        half = jnp.where(guest, 2, jnp.where(x >= 2, 1, 0))
-        return xd, at, half
-
-    targets = [target(xh) for xh in range(HX)]
-
-    def rows_copy(t, i, rows, wait):
-        yh = (y + 4 + i) & 7
-        for xh, (xd, at, half) in enumerate(targets):
-            own = (xd == x) & (yh == y)
-            src = (kpack, vpack0, vpack1)[t].at[yh * HX + xh, pl.ds(0, rows)]
-            dst = region(t, z, c, at, rows)
-
-            @pl.when(jnp.logical_not(own))
-            def _():
-                copy = pltpu.make_async_remote_copy(
-                    src_ref=src, dst_ref=dst, send_sem=p1_send.at[t, i * HX + xh], recv_sem=p1_recv.at[t, half],
-                    device_id=(blk_at(xd), yh), device_id_type=MESH,
-                )
-                copy.wait_send() if wait else copy.start()
-
-            if not wait:
-
-                @pl.when(own)
-                def _():
-                    pltpu.make_async_copy(src, dst, p1_recv.at[t, half]).start()
-
-    def q_copy(i, wait):
-        yh = (y + 4 + i) & 7
-        for xh in range(HX):
-            own = (xh == x) & (yh == y)
-            src = qin.at[:, pl.ds(pl.multiple_of((yh * HX + xh) * HD, HD), HD)]
-            dst = qbuf.at[x, pl.ds(pl.multiple_of(y * PART, 32), PART)]
-
-            @pl.when(jnp.logical_not(own))
-            def _():
-                copy = pltpu.make_async_remote_copy(
-                    src_ref=src, dst_ref=dst, send_sem=p1_send.at[3, i * HX + xh], recv_sem=q_recv.at[0],
-                    device_id=(blk_at(xh), yh), device_id_type=MESH,
-                )
-                copy.wait_send() if wait else copy.start()
-
-            if not wait:
-
-                @pl.when(own)
-                def _():
-                    pltpu.make_async_copy(src, dst, q_recv.at[0]).start()
-
-    def each_y(body):
-        def step(i, _):
-            body(i)
-            return 0
-
-        lax.fori_loop(0, Y, step, 0)
-
-    def all_rows(t, wait):
-        @pl.when(r == 0)
-        def _():
-            each_y(lambda i: rows_copy(t, i, 3, wait))
-
-        @pl.when(r != 0)
-        def _():
-            each_y(lambda i: rows_copy(t, i, 2, wait))
-
-    all_rows(0, False)
 
     def list_copy(j):
         return pltpu.make_async_remote_copy(
@@ -520,10 +527,12 @@
         out_shape=jax.ShapeDtypeStruct(queries.shape, bf),
         in_specs=[
             anywhere, anywhere, anywhere,
-            pl.BlockSpec(memory_space=pltpu.VMEM), pl.BlockSpec(memory_space=pltpu.SMEM),
+            anywhere, anywhere,
         ],
         out_specs=pl.BlockSpec(memory_space=pltpu.VMEM),
         scratch_shapes=[
+            pltpu.VMEM((PER, SEL), jnp.int32),
+            pltpu.SMEM((X * Z * C * PER,), jnp.int32),
             pltpu.VMEM((PART, HEADS * HD), bf),
             pltpu.VMEM((PART, HEADS * HD), bf),
             pltpu.VMEM((PART, HEADS * HD), bf),
@@ -542,7 +551,7 @@
             pltpu.VMEM((24, 128), jnp.int32),
             pltpu.VMEM((X, 24, 128), jnp.int32),
             pltpu.SMEM((X, 24, 128), jnp.int32),
-            dma((3,)),
+            dma((5,)),
             dma((4, HEADS)),
             dma((3, 3)),
             dma((1,)),

time: 127 us -> 126 us (level)
  no operation moved by 1% of the time
where the time goes in v6:
time: 126 us; the launch traced here: 125 us
  Pallas kernels  123 us (98%)
  local copies, waits for them, and re-layouts  1.92 us (2%)
    pallas_call x1, Pallas kernels, local(): pl.pallas_call(kernel, out_shape=jax.ShapeDtypeStruct(queries.shape, bf),...  123 us

profile of v6, /device:TPU:1, one launch (start us, length us, event | category | flops | bytes accessed | tf_op | source)
XLA Modules:
  0.0 125.4 jit_solution(742493366966337435)
XLA Ops:
  0.0 123.5 %shard_map.55 = bf16[96,3072]{1,0:T(8,128)(2,1)} custom-call(bf16[96,3072]{1,0:T(8,128)(2,1)} %q_ref.1, bf16[96,3072]{1,0:T(8,128)(2,1)} %k_ref.1, bf16[96,3072]{1,0:T(8,128)(2,1)} %v_ref.1, s32[6,16]{1,0:T(8,128)} %list_hbm.1, s32[384]{0:T(512)} %fill_hbm.1), custom_call_target="tpu_custom_call" | custom-call | flops 5000000000 | bytes 4000000 | tf_op jit(solution)/shard_map/pallas_call | solution.py:525
  123.5 1.9 %copy.7 = bf16[96,3072]{1,0:T(8,128)(2,1)} copy(bf16[96,3072]{1,0:T(8,128)(2,1)} %shard_map.55) | data formatting | bytes 1179648

commit v7 on v6

--- a/solution.py
+++ b/solution.py
@@ -388,7 +388,7 @@
         both = (EDGE, MID)
 
         def cluster(i):
-            return (x + 1 + (i >> 1)) & 3, i & 1
+            return (x + 1 + (i >> 1)) & 3, (i & 1) ^ (1 - a)
 
         def gather(i, buf):
             xq, s = cluster(i)

time: 126 us -> 126 us (level)
  no operation moved by 1% of the time
where the time goes in v7:
time: 126 us; the launch traced here: 125 us
  Pallas kernels  123 us (98%)
  local copies, waits for them, and re-layouts  1.92 us (2%)
    pallas_call x1, Pallas kernels, local(): pl.pallas_call(kernel, out_shape=jax.ShapeDtypeStruct(queries.shape, bf),...  123 us

profile of v7, /device:TPU:1, one launch (start us, length us, event | category | flops | bytes accessed | tf_op | source)
XLA Modules:
  0.0 125.3 jit_solution(2775497616968653082)
XLA Ops:
  0.0 123.4 %shard_map.55 = bf16[96,3072]{1,0:T(8,128)(2,1)} custom-call(bf16[96,3072]{1,0:T(8,128)(2,1)} %q_ref.1, bf16[96,3072]{1,0:T(8,128)(2,1)} %k_ref.1, bf16[96,3072]{1,0:T(8,128)(2,1)} %v_ref.1, s32[6,16]{1,0:T(8,128)} %list_hbm.1, s32[384]{0:T(512)} %fill_hbm.1), custom_call_target="tpu_custom_call" | custom-call | flops 5000000000 | bytes 4000000 | tf_op jit(solution)/shard_map/pallas_call | solution.py:525
  123.4 1.9 %copy.7 = bf16[96,3072]{1,0:T(8,128)(2,1)} copy(bf16[96,3072]{1,0:T(8,128)(2,1)} %shard_map.55) | data formatting | bytes 1179648
